TPU v7x, 256 devices: a whole 4x4x8 slice. The times are simulated.
256 devices in a mesh: batch: 16 (over z_lo, x, core), seq: 16 (over y, z_hi).
Axes of the slice: x: 4, y: 4, z: 8 (z_hi: 4, z_lo: 2; z = z_hi * 2 + z_lo), core: 2. Of those that a mesh axis runs over, the one named last changes fastest.
Arguments:
- residual: bfloat16 [32768, 4096], P(('batch', 'seq')), may hold values from -25 to 25
- query_proj: bfloat16 [32768, 4096], P(('batch', 'seq')), may hold values from -68 to 68
- key_proj: bfloat16 [32768, 1024], P(('batch', 'seq')), may hold values from -6 to 6
- value_proj: bfloat16 [32768, 1024], P(('batch', 'seq')), may hold values from -6 to 6
- norm_gain: float32 [4096], replicated, may hold values from 0.1 to 1.9
- lengths: int32 [16], P('batch'), may hold values from 512 to 2048, as said below
- positives: int32 [16], replicated, may hold values from 0 to 15, as said below
Outputs:
- batch_loss: float32 [], replicated
- grad_residual: bfloat16 [32768, 4096], P(('batch', 'seq'))
- grad_queries: bfloat16 [32768, 4096], P(('batch', 'seq'))
- grad_keys: bfloat16 [32768, 1024], P(('batch', 'seq'))
- grad_values: bfloat16 [32768, 1024], P(('batch', 'seq'))
Inputs may be any that keep to these rules, and one draw needn't show every extreme that they name: `lengths`: in every draw some document has all 2048 slots valid. `positives`: never the document itself.
All inputs are finite; a program needn't handle non-finite values.
Results may differ from a plain program's by a relative error of at most 0.012.
Values may be sent and summed in bfloat16 or wider, within the bound.
A program may use at most 128 MiB of HBM per device.

v0:
```python
import math

import jax
import jax.numpy as jnp
from jax import lax
from jax.sharding import PartitionSpec as P

HEAD_DIM = 128


TEMP_FACTOR = 10.0
BIAS_SHIFT = -2.0
EPSILON = 1e-06


def siglip_loss(embedding, positives):
    squares = jnp.sum(embedding * embedding, axis=-1, keepdims=True)
    unit_rows = embedding * lax.rsqrt(squares + EPSILON)
    similar = jnp.dot(
        unit_rows, unit_rows.T, precision=lax.Precision.HIGHEST, preferred_element_type=jnp.float32
    )
    logits = TEMP_FACTOR * similar + BIAS_SHIFT
    doc_count = embedding.shape[0]
    labels = jnp.arange(doc_count, dtype=jnp.int32)
    label_signs = jnp.where(labels[None, :] == positives[:, None], 1.0, -1.0).astype(jnp.float32)
    others = labels[None, :] != labels[:, None]
    pair_terms = jnp.where(others, jax.nn.softplus(-label_signs * logits), 0.0)
    return jnp.sum(pair_terms) / doc_count


def head_weights(query_rows, key_rows, valid_mask, factor):
    scores = (
        jnp.einsum("qd,kd->qk", query_rows, key_rows, preferred_element_type=jnp.float32) * factor
    )
    masked = jnp.where(valid_mask[None, :], scores, -jnp.inf)
    row_peak = jnp.max(masked, axis=-1, keepdims=True)
    raw_weights = jnp.where(valid_mask[None, :], jnp.exp(scores - row_peak), 0.0)
    return (raw_weights / jnp.sum(raw_weights, axis=-1, keepdims=True)).astype(jnp.bfloat16)


def on_device(residual, query_proj, key_proj, value_proj, norm_gain, lengths, positives):
    tok_rows, model_width = residual.shape
    kv_width = key_proj.shape[1]
    head_dim = HEAD_DIM
    seq_count = lax.axis_size("seq")
    seq_index = lax.axis_index("seq")
    batch_index = lax.axis_index("batch")
    kv_heads = kv_width // head_dim
    copies = seq_count // kv_heads
    local_heads = model_width // head_dim // seq_count
    group_rows = tok_rows * seq_count
    grad_scale = float(16 * group_rows)
    docs_total = positives.shape[0]
    factor = 1.0 / math.sqrt(head_dim)

    def widen_heads(block):
        spread = jnp.broadcast_to(
            block.reshape(tok_rows, kv_heads, 1, head_dim), (tok_rows, kv_heads, copies, head_dim)
        )
        return spread.reshape(tok_rows, kv_heads * copies * head_dim)

    key_send, value_send = (widen_heads(key_proj), widen_heads(value_proj))
    query_heads, key_heads, value_heads = (
        lax.all_to_all(query_proj, "seq", split_axis=1, concat_axis=0, tiled=True),
        lax.all_to_all(key_send, "seq", split_axis=1, concat_axis=0, tiled=True),
        lax.all_to_all(value_send, "seq", split_axis=1, concat_axis=0, tiled=True),
    )
    query_split = query_heads.reshape(group_rows, local_heads, head_dim).transpose(1, 0, 2)
    length_here = lengths[0]
    valid_mask = jnp.arange(group_rows, dtype=jnp.int32) < length_here

    def forward_head(query_rows):
        weights = head_weights(query_rows, key_heads, valid_mask, factor)
        attended_rows = jnp.dot(weights, value_heads, preferred_element_type=jnp.float32).astype(
            jnp.bfloat16
        )
        return (weights, attended_rows)

    weight_stack, attended_stack = lax.map(forward_head, query_split)
    attended_heads = attended_stack.transpose(1, 0, 2).reshape(group_rows, local_heads * head_dim)
    attended = lax.all_to_all(attended_heads, "seq", split_axis=0, concat_axis=1, tiled=True)
    summed = residual.astype(jnp.float32) + attended.astype(jnp.float32)
    inv_rms = lax.rsqrt(jnp.mean(summed * summed, axis=-1, keepdims=True) + EPSILON)
    scaled_rows = summed * inv_rms
    normed = scaled_rows * norm_gain
    first_token = seq_index * tok_rows
    valid_here = first_token + jnp.arange(tok_rows, dtype=jnp.int32) < length_here
    length_float = length_here.astype(jnp.float32)
    partial_pool = jnp.sum(jnp.where(valid_here[:, None], normed, 0.0), axis=0) / length_float
    all_ids = jnp.arange(docs_total, dtype=jnp.int32)
    doc_table = jnp.where(all_ids[:, None] == batch_index, partial_pool[None, :], 0.0)
    embedding = lax.psum(doc_table, ("batch", "seq"))
    batch_loss, pullback = jax.vjp(lambda emb_rows: siglip_loss(emb_rows, positives), embedding)
    (grad_embedding,) = pullback(jnp.ones((), jnp.float32) * grad_scale)
    grad_row = jnp.sum(jnp.where(all_ids[:, None] == batch_index, grad_embedding, 0.0), axis=0)
    grad_normed = jnp.where(valid_here[:, None], (grad_row / length_float)[None, :], 0.0)
    gained = grad_normed * norm_gain
    grad_summed = inv_rms * (
        gained - scaled_rows * jnp.mean(gained * scaled_rows, axis=-1, keepdims=True)
    )
    grad_residual = grad_summed.astype(jnp.bfloat16)
    grad_heads = lax.all_to_all(grad_residual, "seq", split_axis=1, concat_axis=0, tiled=True)
    grad_split = grad_heads.reshape(group_rows, local_heads, head_dim).transpose(1, 0, 2)

    def backward_head(inputs):
        query_rows, weights, grad_rows = inputs
        weight_float = weights.astype(jnp.float32)
        grad_weights = jnp.einsum(
            "qd,kd->qk", grad_rows, value_heads, preferred_element_type=jnp.float32
        )
        row_dot = jnp.sum(weight_float * grad_weights, axis=-1, keepdims=True)
        grad_scores = (weight_float * (grad_weights - row_dot) * factor).astype(jnp.bfloat16)
        grad_query = jnp.dot(grad_scores, key_heads, preferred_element_type=jnp.float32).astype(
            jnp.bfloat16
        )
        grad_key = jnp.einsum(
            "qk,qd->kd", grad_scores, query_rows, preferred_element_type=jnp.float32
        )
        grad_value = jnp.einsum("qk,qd->kd", weights, grad_rows, preferred_element_type=jnp.float32)
        return (grad_query, grad_key, grad_value)

    query_stack, key_stack, value_stack = lax.map(
        backward_head, (query_split, weight_stack, grad_split)
    )
    grad_query = query_stack.transpose(1, 0, 2).reshape(group_rows, local_heads * head_dim)
    grad_key = jnp.sum(key_stack, axis=0).astype(jnp.bfloat16)
    grad_value = jnp.sum(value_stack, axis=0).astype(jnp.bfloat16)
    query_back, key_back, value_back = (
        lax.all_to_all(grad_query, "seq", split_axis=0, concat_axis=1, tiled=True),
        lax.all_to_all(grad_key, "seq", split_axis=0, concat_axis=1, tiled=True),
        lax.all_to_all(grad_value, "seq", split_axis=0, concat_axis=1, tiled=True),
    )
    key_back = (
        key_back.reshape(tok_rows, kv_heads, copies, head_dim)
        .astype(jnp.float32)
        .sum(axis=2)
        .astype(jnp.bfloat16)
        .reshape(tok_rows, kv_width)
    )
    value_back = (
        value_back.reshape(tok_rows, kv_heads, copies, head_dim)
        .astype(jnp.float32)
        .sum(axis=2)
        .astype(jnp.bfloat16)
        .reshape(tok_rows, kv_width)
    )
    return (batch_loss, grad_residual, query_back, key_back, value_back)


def solution(mesh):
    return jax.shard_map(
        on_device,
        mesh=mesh,
        in_specs=(
            P(("batch", "seq"), None),
            P(("batch", "seq"), None),
            P(("batch", "seq"), None),
            P(("batch", "seq"), None),
            P(),
            P("batch"),
            P(),
        ),
        out_specs=(
            P(),
            P(("batch", "seq"), None),
            P(("batch", "seq"), None),
            P(("batch", "seq"), None),
            P(("batch", "seq"), None),
        ),
        check_vma=False,
    )
```

profile of v0, /device:TPU:8, one launch (start us, length us, event | category | flops | bytes accessed | tf_op | source)
XLA Modules:
  0.0 629.0 jit_solution(13282115090337035113)
XLA Ops:
  9.1 11.6 %all-to-all-start.1 = ((bf16[128,16,128]{2,0,1:T(8,128)(2,1)}), bf16[128,16,128]{2,0,1:T(8,128)(2,1)S(1)}, u32[]{:S(2)}, u32[]{:S(2)}) async-start(bf16[128,16,128]{2,0,1:T(8,128)(2,1)} %bitcast.10), calls=%async_computation.1 | async-start | bytes 1048576 | tf_op jit(solution)/shard_map/all_to_all | solution.py:65
  20.6 2.3 copy.68
  22.9 14.4 %all-to-all-done.1 = bf16[128,16,128]{2,0,1:T(8,128)(2,1)S(1)} async-done(((bf16[128,16,128]{2,0,1:T(8,128)(2,1)}), bf16[128,16,128]{2,0,1:T(8,128)(2,1)S(1)}, u32[]{:S(2)}, u32[]{:S(2)}) %all-to-all-start.1) | async-done | bytes 524320 | tf_op jit(solution)/shard_map/all_to_all | solution.py:65
  37.3 5.0 all-to-all-start
  43.3 26.6 %all-to-all-done = bf16[128,16,256]{0,2,1:T(8,128)(2,1)S(1)} async-done(((bf16[128,16,256]{0,2,1:T(8,128)(2,1)}), bf16[128,16,256]{0,2,1:T(8,128)(2,1)S(1)}, u32[]{:S(2)}, u32[]{:S(2)}) %all-to-all-start) | async-done | bytes 1048608 | tf_op jit(solution)/shard_map/all_to_all | solution.py:64
  70.8 5.8 all-to-all-start.2
  77.8 1.3 copy.72
  79.1 12.1 %all-to-all-done.2 = bf16[128,16,128]{2,0,1:T(8,128)(2,1)S(1)} async-done(((bf16[128,16,128]{2,0,1:T(8,128)(2,1)}), bf16[128,16,128]{2,0,1:T(8,128)(2,1)S(1)}, u32[]{:S(2)}, u32[]{:S(2)}) %all-to-all-start.2) | async-done | bytes 524320 | tf_op jit(solution)/shard_map/all_to_all | solution.py:66
  91.2 1.1 broadcast.82.clone
  92.4 57.9 %while.28 = (s32[]{:T(128)}, bf16[2,2048,2048]{1,2,0:T(8,128)(2,1)}, bf16[2,2048,128]{2,1,0:T(8,128)(2,1)}, bf16[2,2048,128]{2,1,0:T(8,128)(2,1)}, bf16[2048,128...) while((s32[]{:T(128)}, bf16[2,2048,2048]{1,2,0:T(8,128)(2,1)}, ...), condition=%wide.region_3.4_spmd.clone, body=%wide.region_0.3_spmd.clone.sunk | while | flops 2198075392 | bytes 195085520 | solution.py:79
  93.0 3.5 select_reduce_fusion.4
  96.6 4.8 fusion.93
  101.5 7.5 %bitcast_dynamic-update-slice_fusion.2 = (bf16[2,2048,2048]{1,2,0:T(8,128)(2,1)S(1)}, bf16[2048,2048]{0,1:T(8,128)(2,1)}) fusion(bf16[2,2048,2048]{1,2,0:T(8,128)(2,1)S(1)} %bitcast.160, s32[]{:T(128)} %get-tuple-element.374, f32[2048]{0:T(1024)S(1)} %fusion.93, f32[2048]{0:T(1024)S(1)} %get-tuple-element.363, ...), kind=kLoop, calls=%fused_computation.30.clone.1 | loop fusion | flops 20971520 | bytes 33572868 | tf_op jit(solution)/shard_map/while/body/jit(dynamic_update_index_in_dim)/dynamic_update_slice | solution.py:79
  109.0 5.7 copy-done.2
  114.7 6.6 %fusion.94 = bf16[2,2048,128]{2,1,0:T(8,128)(2,1)} fusion(bf16[2,2048,128]{2,1,0:T(8,128)(2,1)} %get-tuple-element.376, s32[]{:T(128)} %get-tuple-element.374, bf16[2048,2048]{0,1:T(8,128)(2,1)} %get-tuple-element.365, bf16[2048,128]{1,0:T(8,128)(2,1)S(1)} %get-tuple-element.387), kind=kOutput, calls=%fused_computation.33.clone.1 | convolution fusion | flops 1074003968 | bytes 9437696 | tf_op jit(solution)/shard_map/while/body/eval_jaxpr/dot_general | solution.py:74
  122.0 3.5 select_reduce_fusion.4
  125.5 4.8 fusion.93
  130.4 7.5 %bitcast_dynamic-update-slice_fusion.2 = (bf16[2,2048,2048]{1,2,0:T(8,128)(2,1)S(1)}, bf16[2048,2048]{0,1:T(8,128)(2,1)}) fusion(bf16[2,2048,2048]{1,2,0:T(8,128)(2,1)S(1)} %bitcast.160, s32[]{:T(128)} %get-tuple-element.374, f32[2048]{0:T(1024)S(1)} %fusion.93, f32[2048]{0:T(1024)S(1)} %get-tuple-element.363, ...), kind=kLoop, calls=%fused_computation.30.clone.1 | loop fusion | flops 20971520 | bytes 33572868 | tf_op jit(solution)/shard_map/while/body/jit(dynamic_update_index_in_dim)/dynamic_update_slice | solution.py:79
  137.9 5.7 copy-done.2
  143.7 6.6 %fusion.94 = bf16[2,2048,128]{2,1,0:T(8,128)(2,1)} fusion(bf16[2,2048,128]{2,1,0:T(8,128)(2,1)} %get-tuple-element.376, s32[]{:T(128)} %get-tuple-element.374, bf16[2048,2048]{0,1:T(8,128)(2,1)} %get-tuple-element.365, bf16[2048,128]{1,0:T(8,128)(2,1)S(1)} %get-tuple-element.387), kind=kOutput, calls=%fused_computation.33.clone.1 | convolution fusion | flops 1074003968 | bytes 9437696 | tf_op jit(solution)/shard_map/while/body/eval_jaxpr/dot_general | solution.py:74
  150.2 1.5 copy.73
  152.0 1.2 copy.74
  153.2 6.0 all-to-all-start.3
  160.1 1.6 copy.67
  161.8 22.8 %all-to-all-done.3 = bf16[16,128,256]{1,2,0:T(8,128)(2,1)S(1)} async-done(((bf16[16,128,256]{1,2,0:T(8,128)(2,1)}), bf16[16,128,256]{1,2,0:T(8,128)(2,1)S(1)}, u32[]{:S(2)}, u32[]{:S(2)}) %all-to-all-start.3) | async-done | bytes 1048608 | tf_op jit(solution)/shard_map/all_to_all | solution.py:81
  185.2 1.3 select_reduce_fusion.1
  187.3 247.6 %all-reduce.2.cloned.1.call-done = f32[16,4096]{1,0:T(8,128)} async-done(((f32[16,4096]{1,0:T(8,128)}), f32[16,4096]{1,0:T(8,128)}) %all-reduce.2.cloned.1.call-update) | async-done | bytes 262160 | tf_op jit(solution)/shard_map/psum | solution.py:92
  434.9 1.1 multiply_reduce_fusion.3
  436.0 2.2 select_reduce_fusion.2
  438.2 1.4 fusion.39
  439.6 1.6 multiply_reduce_fusion.2
  441.3 1.1 fusion.37
  442.4 1.3 multiply_reduce_fusion
  443.7 2.0 multiply_convert_fusion
  445.7 8.1 %all-to-all-start.4 = ((bf16[128,16,256]{0,2,1:T(8,128)(2,1)}), bf16[128,16,256]{0,2,1:T(8,128)(2,1)S(1)}, u32[]{:S(2)}, u32[]{:S(2)}) async-start(bf16[128,16,256]{0,2,1:T(8,128)(2,1)} %bitcast.166), calls=%async_computation.4 | async-start | bytes 2097152 | tf_op jit(solution)/shard_map/all_to_all | solution.py:102
  453.8 27.3 %all-to-all-done.4 = bf16[128,16,256]{0,2,1:T(8,128)(2,1)S(1)} async-done(((bf16[128,16,256]{0,2,1:T(8,128)(2,1)}), bf16[128,16,256]{0,2,1:T(8,128)(2,1)S(1)}, u32[]{:S(2)}, u32[]{:S(2)}) %all-to-all-start.4) | async-done | bytes 1048608 | tf_op jit(solution)/shard_map/all_to_all | solution.py:102
  481.1 1.7 copy.75
  482.7 1.5 reshape.122
  484.2 1.2 broadcast.82
  485.4 57.6 %while.27 = (s32[]{:T(128)}, bf16[2,2048,128]{2,1,0:T(8,128)(2,1)}, f32[2,2048,128]{2,1,0:T(8,128)}, f32[2,2048,128]{2,1,0:T(8,128)}, bf16[2,2048,2048]{1,2,0:T(...) while((s32[]{:T(128)}, bf16[2,2048,128]{2,1,0:T(8,128)(2,1)}, ...), condition=%wide.region_14.15_spmd, body=%wide.region_12.14_spmd.sunk | while | flops 4328781824 | bytes 181423936 | solution.py:122
  485.4 4.7 fusion.85
  490.2 9.9 %fusion.86 = bf16[2048,2048]{0,1:T(8,128)(2,1)} fusion(f32[2048,2048]{0,1:T(8,128)S(1)} %get-tuple-element.353, f32[2048]{0:T(1024)S(1)} %get-tuple-element.354, bf16[2,2048,2048]{1,2,0:T(8,128)(2,1)} %get-tuple-element.414, s32[]{:T(128)} %get-tuple-element.400), kind=kLoop, calls=%fused_computation.5.clone.1 | loop fusion | flops 20971520 | bytes 33562628 | tf_op jit(solution)/shard_map/while/body/eval_jaxpr/convert_element_type | solution.py:112
  500.1 7.0 %fusion.88 = f32[2,2048,128]{2,1,0:T(8,128)} fusion(f32[2,2048,128]{2,1,0:T(8,128)} %get-tuple-element.402, s32[]{:T(128)} %get-tuple-element.400, bf16[2048,2048]{0,1:T(8,128)(2,1)} %fusion.86, bf16[2,2048,128]{2,1,0:T(8,128)(2,1)} %get-tuple-element.418), kind=kOutput, calls=%fused_computation.10.clone.1 | convolution fusion | flops 1073741824 | bytes 9962496 | tf_op jit(solution)/shard_map/while/body/eval_jaxpr/qk,qd->kd/dot_general | solution.py:116
  507.1 2.7 fusion.87
  510.8 3.4 fusion.89
  514.2 4.7 fusion.85
  519.0 9.9 %fusion.86 = bf16[2048,2048]{0,1:T(8,128)(2,1)} fusion(f32[2048,2048]{0,1:T(8,128)S(1)} %get-tuple-element.353, f32[2048]{0:T(1024)S(1)} %get-tuple-element.354, bf16[2,2048,2048]{1,2,0:T(8,128)(2,1)} %get-tuple-element.414, s32[]{:T(128)} %get-tuple-element.400), kind=kLoop, calls=%fused_computation.5.clone.1 | loop fusion | flops 20971520 | bytes 33562628 | tf_op jit(solution)/shard_map/while/body/eval_jaxpr/convert_element_type | solution.py:112
  528.9 6.9 %fusion.88 = f32[2,2048,128]{2,1,0:T(8,128)} fusion(f32[2,2048,128]{2,1,0:T(8,128)} %get-tuple-element.402, s32[]{:T(128)} %get-tuple-element.400, bf16[2048,2048]{0,1:T(8,128)(2,1)} %fusion.86, bf16[2,2048,128]{2,1,0:T(8,128)(2,1)} %get-tuple-element.418), kind=kOutput, calls=%fused_computation.10.clone.1 | convolution fusion | flops 1073741824 | bytes 9962496 | tf_op jit(solution)/shard_map/while/body/eval_jaxpr/qk,qd->kd/dot_general | solution.py:116
  535.8 2.7 fusion.87
  538.5 1.0 copy-done.6
  539.6 3.4 fusion.89
  543.0 2.8 reduce_sum.134
  545.7 6.7 %all-to-all-start.6 = ((bf16[16,128,128]{2,1,0:T(8,128)(2,1)}), bf16[16,128,128]{2,1,0:T(8,128)(2,1)S(1)}, u32[]{:S(2)}, u32[]{:S(2)}) async-start(bf16[16,128,128]{2,1,0:T(8,128)(2,1)} %bitcast.27), calls=%async_computation.6 | async-start | bytes 1048576 | tf_op jit(solution)/shard_map/all_to_all | solution.py:130
  552.4 2.7 reduce_sum.136
  555.1 13.1 %all-to-all-done.6 = bf16[16,128,128]{2,1,0:T(8,128)(2,1)S(1)} async-done(((bf16[16,128,128]{2,1,0:T(8,128)(2,1)}), bf16[16,128,128]{2,1,0:T(8,128)(2,1)S(1)}, u32[]{:S(2)}, u32[]{:S(2)}) %all-to-all-start.6) | async-done | bytes 524320 | tf_op jit(solution)/shard_map/all_to_all | solution.py:130
  568.2 6.5 %all-to-all-start.7 = ((bf16[16,128,128]{2,1,0:T(8,128)(2,1)}), bf16[16,128,128]{2,1,0:T(8,128)(2,1)}, u32[]{:S(2)}, u32[]{:S(2)}) async-start(bf16[16,128,128]{2,1,0:T(8,128)(2,1)} %bitcast.31), calls=%async_computation.7 | async-start | bytes 1048576 | tf_op jit(solution)/shard_map/all_to_all | solution.py:131
  574.7 1.5 copy.78
  576.5 1.2 copy.79
  577.7 11.8 %all-to-all-done.7 = bf16[16,128,128]{2,1,0:T(8,128)(2,1)} async-done(((bf16[16,128,128]{2,1,0:T(8,128)(2,1)}), bf16[16,128,128]{2,1,0:T(8,128)(2,1)}, u32[]{:S(2)}, u32[]{:S(2)}) %all-to-all-start.7) | async-done | bytes 524320 | tf_op jit(solution)/shard_map/all_to_all | solution.py:131
  589.5 6.1 all-to-all-start.5
  595.7 1.3 copy.82
  598.8 1.1 bitcast_reduce_fusion
  600.9 18.8 %all-to-all-done.5 = bf16[16,128,256]{1,2,0:T(8,128)(2,1)S(1)} async-done(((bf16[16,128,256]{1,2,0:T(8,128)(2,1)}), bf16[16,128,256]{1,2,0:T(8,128)(2,1)S(1)}, u32[]{:S(2)}, u32[]{:S(2)}) %all-to-all-start.5) | async-done | bytes 1048608 | tf_op jit(solution)/shard_map/all_to_all | solution.py:129
  619.7 1.3 copy.83
  (89 shorter events, 11.6 us)
Async XLA Ops:
  7.2 1.0 copy-start
  9.1 28.2 %all-to-all-start.1 = ((bf16[128,16,128]{2,0,1:T(8,128)(2,1)}), bf16[128,16,128]{2,0,1:T(8,128)(2,1)S(1)}, u32[]{:S(2)}, u32[]{:S(2)}) async-start(bf16[128,16,128]{2,0,1:T(8,128)(2,1)} %bitcast.10), calls=%async_computation.1 | async-start | bytes 1048576 | tf_op jit(solution)/shard_map/all_to_all | solution.py:65
  37.3 32.6 %all-to-all-start = ((bf16[128,16,256]{0,2,1:T(8,128)(2,1)}), bf16[128,16,256]{0,2,1:T(8,128)(2,1)S(1)}, u32[]{:S(2)}, u32[]{:S(2)}) async-start(bf16[128,16,256]{0,2,1:T(8,128)(2,1)} %bitcast.7), calls=%async_computation | async-start | bytes 2097152 | tf_op jit(solution)/shard_map/all_to_all | solution.py:64
  70.8 20.4 %all-to-all-start.2 = ((bf16[128,16,128]{2,0,1:T(8,128)(2,1)}), bf16[128,16,128]{2,0,1:T(8,128)(2,1)S(1)}, u32[]{:S(2)}, u32[]{:S(2)}) async-start(bf16[128,16,128]{2,0,1:T(8,128)(2,1)} %bitcast.13), calls=%async_computation.2 | async-start | bytes 1048576 | tf_op jit(solution)/shard_map/all_to_all | solution.py:66
  93.0 8.4 %slice-start = ((s8[16777216]{0:T(1024)(128)(4,1)}), s8[4194304]{0:T(1024)(128)(4,1)S(1)}, s32[]{:S(2)}) async-start(s8[16777216]{0:T(1024)(128)(4,1)} %bitcast.159), calls=%async_computation.9 | async-start | bytes 8388608 | tf_op jit(solution)/shard_map/while
  93.0 8.4 %slice-start.1 = ((s8[16777216]{0:T(1024)(128)(4,1)}), s8[4194304]{0:T(1024)(128)(4,1)S(1)}, s32[]{:S(2)}) async-start(s8[16777216]{0:T(1024)(128)(4,1)} %bitcast.159), calls=%async_computation.10 | async-start | bytes 8388608 | tf_op jit(solution)/shard_map/while
  93.0 8.4 %slice-start.2 = ((s8[16777216]{0:T(1024)(128)(4,1)}), s8[4194304]{0:T(1024)(128)(4,1)S(1)}, s32[]{:S(2)}) async-start(s8[16777216]{0:T(1024)(128)(4,1)} %bitcast.159), calls=%async_computation.11 | async-start | bytes 8388608 | tf_op jit(solution)/shard_map/while
  96.6 4.9 slice-start.3
  109.0 5.7 copy-start.2
  121.9 8.4 %slice-start = ((s8[16777216]{0:T(1024)(128)(4,1)}), s8[4194304]{0:T(1024)(128)(4,1)S(1)}, s32[]{:S(2)}) async-start(s8[16777216]{0:T(1024)(128)(4,1)} %bitcast.159), calls=%async_computation.9 | async-start | bytes 8388608 | tf_op jit(solution)/shard_map/while
  122.0 8.4 %slice-start.1 = ((s8[16777216]{0:T(1024)(128)(4,1)}), s8[4194304]{0:T(1024)(128)(4,1)S(1)}, s32[]{:S(2)}) async-start(s8[16777216]{0:T(1024)(128)(4,1)} %bitcast.159), calls=%async_computation.10 | async-start | bytes 8388608 | tf_op jit(solution)/shard_map/while
  122.0 8.4 %slice-start.2 = ((s8[16777216]{0:T(1024)(128)(4,1)}), s8[4194304]{0:T(1024)(128)(4,1)S(1)}, s32[]{:S(2)}) async-start(s8[16777216]{0:T(1024)(128)(4,1)} %bitcast.159), calls=%async_computation.11 | async-start | bytes 8388608 | tf_op jit(solution)/shard_map/while
  125.5 4.9 slice-start.3
  137.9 5.7 copy-start.2
  150.2 34.9 %copy-start.7 = (f32[4096]{0:T(1024)S(1)}, f32[4096]{0:T(1024)}, u32[]{:S(2)}) copy-start(f32[4096]{0:T(1024)} %param.15) | copy-start | bytes 49156
  150.2 285.8 %copy-start.8 = (s32[16]{0:T(128)S(1)}, s32[16]{0:T(128)}, u32[]{:S(2)}) copy-start(s32[16]{0:T(128)} %param.17) | copy-start | bytes 196
  153.2 31.4 %all-to-all-start.3 = ((bf16[16,128,256]{1,2,0:T(8,128)(2,1)}), bf16[16,128,256]{1,2,0:T(8,128)(2,1)S(1)}, u32[]{:S(2)}, u32[]{:S(2)}) async-start(bf16[16,128,256]{1,2,0:T(8,128)(2,1)} %copy.74), calls=%async_computation.3 | async-start | bytes 2097152 | tf_op jit(solution)/shard_map/all_to_all | solution.py:81
  159.3 275.6 %all-reduce.2.cloned.1.call-start = ((), (), s32[]{:S(2)}) async-start(), calls=%async_computation.8 | async-start | bytes 524288 | tf_op jit(solution)/shard_map/psum | solution.py:92
  445.7 35.4 %all-to-all-start.4 = ((bf16[128,16,256]{0,2,1:T(8,128)(2,1)}), bf16[128,16,256]{0,2,1:T(8,128)(2,1)S(1)}, u32[]{:S(2)}, u32[]{:S(2)}) async-start(bf16[128,16,256]{0,2,1:T(8,128)(2,1)} %bitcast.166), calls=%async_computation.4 | async-start | bytes 2097152 | tf_op jit(solution)/shard_map/all_to_all | solution.py:102
  490.2 20.6 %slice-start.4 = ((s8[16777216]{0:T(1024)(128)(4,1)}), s8[4194304]{0:T(1024)(128)(4,1)S(1)}, s32[]{:S(2)}) async-start(s8[16777216]{0:T(1024)(128)(4,1)} %bitcast.161), calls=%async_computation.13 | async-start | bytes 8388608 | tf_op jit(solution)/shard_map/while
  490.2 20.6 %slice-start.5 = ((s8[16777216]{0:T(1024)(128)(4,1)}), s8[4194304]{0:T(1024)(128)(4,1)S(1)}, s32[]{:S(2)}) async-start(s8[16777216]{0:T(1024)(128)(4,1)} %bitcast.161), calls=%async_computation.14 | async-start | bytes 8388608 | tf_op jit(solution)/shard_map/while
  490.2 20.6 %slice-start.6 = ((s8[16777216]{0:T(1024)(128)(4,1)}), s8[4194304]{0:T(1024)(128)(4,1)S(1)}, s32[]{:S(2)}) async-start(s8[16777216]{0:T(1024)(128)(4,1)} %bitcast.161), calls=%async_computation.15 | async-start | bytes 8388608 | tf_op jit(solution)/shard_map/while
  500.1 7.0 %copy-start.3 = (bf16[2048,2048]{0,1:T(8,128)(2,1)S(1)}, bf16[2048,2048]{0,1:T(8,128)(2,1)}, u32[]{:S(2)}) copy-start(bf16[2048,2048]{0,1:T(8,128)(2,1)} %fusion.86) | copy-start | bytes 25165828 | tf_op jit(solution)/shard_map/while
  500.1 7.0 %copy-start.5 = (bf16[2,2048,128]{2,1,0:T(8,128)(2,1)S(1)}, bf16[2,2048,128]{2,1,0:T(8,128)(2,1)}, u32[]{:S(2)}) copy-start(bf16[2,2048,128]{2,1,0:T(8,128)(2,1)} %get-tuple-element.401) | copy-start | bytes 3145732 | tf_op jit(solution)/shard_map/while
  500.1 10.7 %slice-start.7 = ((s8[16777216]{0:T(1024)(128)(4,1)}), s8[4194304]{0:T(1024)(128)(4,1)S(1)}, s32[]{:S(2)}) async-start(s8[16777216]{0:T(1024)(128)(4,1)} %bitcast.161), calls=%async_computation.16 | async-start | bytes 8388608 | tf_op jit(solution)/shard_map/while
  509.8 1.0 copy-start.6
  519.0 20.6 %slice-start.4 = ((s8[16777216]{0:T(1024)(128)(4,1)}), s8[4194304]{0:T(1024)(128)(4,1)S(1)}, s32[]{:S(2)}) async-start(s8[16777216]{0:T(1024)(128)(4,1)} %bitcast.161), calls=%async_computation.13 | async-start | bytes 8388608 | tf_op jit(solution)/shard_map/while
  519.0 20.6 %slice-start.5 = ((s8[16777216]{0:T(1024)(128)(4,1)}), s8[4194304]{0:T(1024)(128)(4,1)S(1)}, s32[]{:S(2)}) async-start(s8[16777216]{0:T(1024)(128)(4,1)} %bitcast.161), calls=%async_computation.14 | async-start | bytes 8388608 | tf_op jit(solution)/shard_map/while
  519.0 20.6 %slice-start.6 = ((s8[16777216]{0:T(1024)(128)(4,1)}), s8[4194304]{0:T(1024)(128)(4,1)S(1)}, s32[]{:S(2)}) async-start(s8[16777216]{0:T(1024)(128)(4,1)} %bitcast.161), calls=%async_computation.15 | async-start | bytes 8388608 | tf_op jit(solution)/shard_map/while
  528.9 6.9 %copy-start.3 = (bf16[2048,2048]{0,1:T(8,128)(2,1)S(1)}, bf16[2048,2048]{0,1:T(8,128)(2,1)}, u32[]{:S(2)}) copy-start(bf16[2048,2048]{0,1:T(8,128)(2,1)} %fusion.86) | copy-start | bytes 25165828 | tf_op jit(solution)/shard_map/while
  528.9 6.9 %copy-start.5 = (bf16[2,2048,128]{2,1,0:T(8,128)(2,1)S(1)}, bf16[2,2048,128]{2,1,0:T(8,128)(2,1)}, u32[]{:S(2)}) copy-start(bf16[2,2048,128]{2,1,0:T(8,128)(2,1)} %get-tuple-element.401) | copy-start | bytes 3145732 | tf_op jit(solution)/shard_map/while
  528.9 10.6 %slice-start.7 = ((s8[16777216]{0:T(1024)(128)(4,1)}), s8[4194304]{0:T(1024)(128)(4,1)S(1)}, s32[]{:S(2)}) async-start(s8[16777216]{0:T(1024)(128)(4,1)} %bitcast.161), calls=%async_computation.16 | async-start | bytes 8388608 | tf_op jit(solution)/shard_map/while
  538.5 1.0 copy-start.6
  543.0 52.7 %copy-start.4 = (bf16[128,4096]{0,1:T(8,128)(2,1)S(1)}, bf16[128,4096]{0,1:T(8,128)(2,1)}, u32[]{:S(2)}) copy-start(bf16[128,4096]{0,1:T(8,128)(2,1)} %multiply_convert_fusion) | copy-start | bytes 3145732
  545.7 22.4 %all-to-all-start.6 = ((bf16[16,128,128]{2,1,0:T(8,128)(2,1)}), bf16[16,128,128]{2,1,0:T(8,128)(2,1)S(1)}, u32[]{:S(2)}, u32[]{:S(2)}) async-start(bf16[16,128,128]{2,1,0:T(8,128)(2,1)} %bitcast.27), calls=%async_computation.6 | async-start | bytes 1048576 | tf_op jit(solution)/shard_map/all_to_all | solution.py:130
  568.2 21.4 %all-to-all-start.7 = ((bf16[16,128,128]{2,1,0:T(8,128)(2,1)}), bf16[16,128,128]{2,1,0:T(8,128)(2,1)}, u32[]{:S(2)}, u32[]{:S(2)}) async-start(bf16[16,128,128]{2,1,0:T(8,128)(2,1)} %bitcast.31), calls=%async_computation.7 | async-start | bytes 1048576 | tf_op jit(solution)/shard_map/all_to_all | solution.py:131
  574.7 46.3 %copy-start.1 = (bf16[128,1024]{1,0:T(8,128)(2,1)S(1)}, bf16[128,1024]{1,0:T(8,128)(2,1)}, u32[]{:S(2)}) copy-start(bf16[128,1024]{1,0:T(8,128)(2,1)} %param.13) | copy-start | bytes 786436
  589.5 30.1 %all-to-all-start.5 = ((bf16[16,128,256]{1,2,0:T(8,128)(2,1)}), bf16[16,128,256]{1,2,0:T(8,128)(2,1)S(1)}, u32[]{:S(2)}, u32[]{:S(2)}) async-start(bf16[16,128,256]{1,2,0:T(8,128)(2,1)} %copy.79), calls=%async_computation.5 | async-start | bytes 2097152 | tf_op jit(solution)/shard_map/all_to_all | solution.py:129
Sparse Core Ops, SparseCore 0:
  187.4 247.4 all-reduce.1
where the time goes:
time: 631 us; the launch traced here: 629 us
  waiting for transfers between devices  395 us (63%)
  matrix products  61 us (10%)
  other arithmetic  60.6 us (10%)
  starting transfers between devices  56 us (9%)
  local copies, waits for them, and re-layouts  39.9 us (6%)
  between operations  16.7 us (3%)
    psum x1, waiting for transfers between devices, on_device(): embedding = lax.psum(doc_table, ('batch', 'seq'))  248 us
    all_to_all x1, waiting for transfers between devices, on_device(): lax.all_to_all(grad_residual, 'seq', split_axis=1, concat_axis=0, tiled=T...  27.3 us
    all_to_all x1, waiting for transfers between devices, on_device(): lax.all_to_all(query_proj, 'seq', split_axis=1, concat_axis=0, tiled=True)  26.6 us
    all_to_all x1, waiting for transfers between devices, on_device(): lax.all_to_all(attended_heads, 'seq', split_axis=0, concat_axis=1, tiled=...  22.8 us
    convert_element_type x2, other arithmetic, backward_head(): (weight_float * (grad_weights - row_dot) * factor).astype(jnp.bfloat16)  19.8 us
    all_to_all x1, waiting for transfers between devices, on_device(): lax.all_to_all(grad_query, 'seq', split_axis=0, concat_axis=1, tiled=True)  18.8 us
    dynamic_update_slice x2, other arithmetic, on_device(): weight_stack, attended_stack = lax.map(forward_head, query_split)  15 us
    all_to_all x1, waiting for transfers between devices, on_device(): lax.all_to_all(key_send, 'seq', split_axis=1, concat_axis=0, tiled=True)  14.4 us
  transfers between devices with their start and end apart: 9, of which 9 were waited for; matrix products, arithmetic and copies ran while one was open for 3% of the time, Pallas kernels for 0%

commit v1 on v0

v1 whole, which is shorter than its diff:
```python
import functools
import math

import jax
import jax.numpy as jnp
from jax import lax
from jax.experimental import pallas as pl
from jax.experimental.pallas import tpu as pltpu
from jax.sharding import PartitionSpec as P

MESH = pl.DeviceIdType.MESH
HD = 128
NY = 4
NZ = 4
H = 2
G = 4
GW = G * HD
EPS = 1e-6
F32 = jnp.float32
BF16 = jnp.bfloat16
FACTOR = 1.0 / math.sqrt(HD)
LOG2E_FACTOR = FACTOR * math.log2(math.e)


def dot(a, b, dims=((1,), (0,))):
    return lax.dot_general(a, b, (dims, ((), ())), preferred_element_type=F32)


def kernel(
    nb, t_rows,
    len_ref, pos_ref, res_hbm, q_hbm, k_hbm, v_hbm, gain_ref,
    loss_ref, out_gr, out_gq, out_gk, out_gv,
    kvb, kfx, kzt, vta, qin, qs, qt, est, mb, mrun, linv, acc, ato, ati, res, sm,
    pp, ppa, emba, gref, gro, doi, dot_t, dqa, gqo, dka, dva, dkvo, own, rs1, rs2, fin,
    kvs, kvr, kvl, qss, qsr, qsl, z1s, z1r, z2s, z2r, ats, atr, atl, resl,
    p1s, p1r, p2s, p2r, grs, grr, grl, gol, r1s, r1r, r2s, r2r, gqs, gqr, gql, gks, gkr, gkl,
):
    T = t_rows
    BK = NY * T
    ns = NY * NZ
    b = lax.axis_index("batch")
    s = lax.axis_index("seq")
    y = lax.div(s, NZ)
    zh = lax.rem(s, NZ)
    zr = lax.rem(zh + 1, NZ)
    zl = lax.rem(zh + NZ - 1, NZ)
    right = (b, y * NZ + zr)
    left = (b, y * NZ + zl)

    def yo(k):
        return lax.rem(y + k, NY)

    def ydev(yy):
        return (b, yy * NZ + zh)

    def col(index, width):
        return pl.ds(pl.multiple_of(index * width, width), width)

    def rcopy(src, dst, ssem, rsem, dev):
        return pltpu.make_async_remote_copy(
            src_ref=src, dst_ref=dst, send_sem=ssem, recv_sem=rsem, device_id=dev, device_id_type=MESH
        )

    def lcopy(src, dst, sem):
        return pltpu.make_async_copy(src, dst, sem)

    def await_ref(ref, sem):
        pltpu.make_async_copy(ref, ref, sem).wait()

    sends = []

    def send(src, dst, ssem, rsem, dev):
        copy = rcopy(src, dst, ssem, rsem, dev)
        copy.start()
        sends.append(copy)

    length = len_ref[0]
    lenf = length.astype(F32)

    res_copy = lcopy(res_hbm, res, resl)
    res_copy.start()
    for h in range(H):
        for c, src in ((0, k_hbm), (1, v_hbm)):
            lcopy(src.at[:, col(2 * y + h, HD)], kvb.at[h, 0, c, y], kvl.at[h, c]).start()
        lcopy(q_hbm.at[:, col(2 * y + h, GW)], qin.at[h, y], qsl.at[h]).start()

    barrier = pltpu.get_barrier_semaphore()
    for k in range(1, ns):
        pl.semaphore_signal(barrier, inc=1, device_id=(b, lax.rem(s + k, ns)), device_id_type=MESH)
    for k in range(1, nb):
        pl.semaphore_signal(barrier, inc=1, device_id=(lax.rem(b + k, nb), s), device_id_type=MESH)
    pl.semaphore_wait(barrier, ns - 1 + nb - 1)

    for h in range(H):
        for k in (1, 3, 2):
            yy = yo(k)
            for c, src in ((0, k_hbm), (1, v_hbm)):
                send(src.at[:, col(2 * yy + h, HD)], kvb.at[h, 0, c, y], kvs.at[h, c, k - 1], kvr.at[h, c, k - 1], ydev(yy))
    for h in range(H):
        for k in (1, 3, 2):
            yy = yo(k)
            send(q_hbm.at[:, col(2 * yy + h, GW)], qin.at[h, y], qss.at[h, k - 1], qsr.at[h, k - 1], ydev(yy))

    for h in range(H):
        for k in (0, 1, 3, 2):
            p = yo(NY - k)
            for c, src in ((0, k_hbm), (1, v_hbm)):
                if k == 0:
                    lcopy(src.at[:, col(2 * y + h, HD)], kvb.at[h, 0, c, y], kvl.at[h, c]).wait()
                else:
                    await_ref(kvb.at[h, 0, c, p], kvr.at[h, c, k - 1])
            send(kvb.at[h, 0, :, p], kvb.at[h, 1, :, p], z1s.at[h, 0, k], z1r.at[h, 0, k], right)
            send(kvb.at[h, 0, :, p], kvb.at[h, 2, :, p], z1s.at[h, 1, k], z1r.at[h, 1, k], left)

    def hop2(h, way):
        src, dev, piece = (1, right, 0) if way == 0 else (2, left, 2)
        return rcopy(
            kvb.at[h, src, :, pl.ds(piece, 2)], kvb.at[h, 3, :, pl.ds(piece, 2)], z2s.at[h, way], z2r.at[h, way], dev
        )

    def att_send(h, kk):
        yy = yo(kk)
        return rcopy(ato.at[h, yy], ati.at[h, y], ats.at[h, kk - 1], atr.at[h, kk - 1], ydev(yy))

    def fwd_step(step, carry):
        rel = lax.div(step, H)
        h = lax.rem(step, H)

        @pl.when(rel == 0)
        def _():
            for k in range(NY):
                if k == 0:
                    lcopy(q_hbm.at[:, col(2 * y + h, GW)], qin.at[h, y], qsl.at[h]).wait()
                else:
                    await_ref(qin.at[h, yo(NY - k)], qsr.at[h, k - 1])

            def prep_q(yy, carry):
                for j in range(G):
                    head = qin[h, yy, :, j * HD : (j + 1) * HD]
                    qs[h, yy, j * T : (j + 1) * T, :] = head
                    qt[h, yy, :, j * T : (j + 1) * T] = head.astype(F32).T.astype(BF16)
                mrun[h, yy] = jnp.full((1, G * T), -3e38, F32)
                acc[h, yy] = jnp.zeros((HD + 16, G * T), F32)
                return carry

            lax.fori_loop(0, NY, prep_q, 0)

        @pl.when(rel == 1)
        def _():
            for k in range(NY):
                await_ref(kvb.at[h, 1, :, yo(NY - k)], z1r.at[h, 0, k])
            hop2(h, 0).start()

        @pl.when(rel == 2)
        def _():
            for k in range(NY):
                await_ref(kvb.at[h, 2, :, yo(NY - k)], z1r.at[h, 1, k])
            hop2(h, 1).start()

        @pl.when(rel == 3)
        def _():
            await_ref(kvb.at[h, 3, :, pl.ds(0, 2)], z2r.at[h, 0])
            await_ref(kvb.at[h, 3, :, pl.ds(2, 2)], z2r.at[h, 1])

        zb = lax.rem(zh + jnp.where(rel == 0, 0, jnp.where(rel == 1, 3, jnp.where(rel == 2, 1, 2))), NZ)
        first_key = kvb[h, rel, 0, 0, 0:1, :].astype(F32)
        for yy in range(NY):
            base = (yy * NZ + zb) * T
            valid = lax.broadcasted_iota(jnp.int32, (T, HD), 0) + base < length
            rows = slice(yy * T, (yy + 1) * T)
            kp = kvb[h, rel, 0, yy].astype(F32)
            vp = kvb[h, rel, 1, yy].astype(F32)
            kfx[h, rel, rows, :] = jnp.where(valid, kp, first_key).astype(BF16)
            kzt[h, rel, :, rows] = jnp.where(valid, kp, 0.0).T.astype(BF16)
            vta[h, rel, 0:HD, rows] = jnp.where(valid, vp, 0.0).T.astype(BF16)
            lanes = lax.broadcasted_iota(jnp.int32, (16, T), 1) + base < length
            vta[h, rel, HD : HD + 16, rows] = jnp.where(lanes, 1.0, 0.0).astype(BF16)

        def chunk(t, carry):
            kk = lax.rem(t + 1, NY)
            yy = yo(kk)
            half = G * T // 2
            for part in range(2):
                lanes = slice(part * half, (part + 1) * half)
                sc = dot(kfx[h, rel], qt[h, yy, :, lanes])
                m = jnp.max(sc, axis=0, keepdims=True)
                e = jnp.exp2((sc - m) * LOG2E_FACTOR).astype(BF16)
                est[h, rel, yy, :, lanes] = e
                mb[h, rel, yy, :, lanes] = m
                o = dot(vta[h, rel], e)
                mo = mrun[h, yy, :, lanes]
                mn = jnp.maximum(mo, m)
                keep = jnp.exp2((mo - mn) * LOG2E_FACTOR)
                add = jnp.exp2((m - mn) * LOG2E_FACTOR)
                acc[h, yy, :, lanes] = acc[h, yy, :, lanes] * keep + o * add
                mrun[h, yy, :, lanes] = mn

            @pl.when(rel == 3)
            def _():
                li = 1.0 / acc[h, yy, HD : HD + 1, :]
                linv[h, yy] = li
                o = acc[h, yy, 0:HD, :] * li
                acc[h, yy, 0:HD, :] = o
                for j in range(G):
                    ato[h, yy, :, j * HD : (j + 1) * HD] = o[:, j * T : (j + 1) * T].T.astype(BF16)

                @pl.when(kk > 0)
                def _():
                    att_send(h, kk).start()

                @pl.when(kk == 0)
                def _():
                    lcopy(ato.at[h, y], ati.at[h, y], atl.at[h]).start()

            return carry

        lax.fori_loop(0, NY, chunk, 0)
        return carry

    lax.fori_loop(0, NZ * H, fwd_step, 0)

    res_copy.wait()
    for h in range(H):
        lcopy(ato.at[h, y], ati.at[h, y], atl.at[h]).wait()
        for k in range(1, NY):
            await_ref(ati.at[h, yo(NY - k)], atr.at[h, k - 1])
    square = jnp.zeros((T, HD), F32)
    for g in range(NY * H):
        x = res[:, g * GW : (g + 1) * GW].astype(F32) + ati[g % H, g // H].astype(F32)
        sm[g] = x
        x = x * x
        for j in range(G):
            square = square + x[:, j * HD : (j + 1) * HD]
    inv = lax.rsqrt(jnp.sum(square, axis=1, keepdims=True) * (1.0 / (NY * H * GW)) + EPS)
    valid_row = lax.broadcasted_iota(jnp.int32, (T, GW), 0) + s * T < length
    for g in range(NY * H):
        scaled = sm[g] * inv
        sm[g] = scaled
        normed = scaled * gain_ref[0:1, g * GW : (g + 1) * GW]
        pp[g : g + 1, :] = jnp.sum(jnp.where(valid_row, normed, 0.0), axis=0, keepdims=True) / lenf

    for k in range(1, ns):
        send(pp, ppa.at[s], p1s.at[k - 1], p1r.at[k - 1], (b, lax.rem(s + k, ns)))
    ppa[s] = pp[...]
    for k in range(1, ns):
        await_ref(ppa.at[lax.rem(s + ns - k, ns)], p1r.at[k - 1])
    mine = ppa[0]
    for i in range(1, ns):
        mine = mine + ppa[i]
    emba[b] = mine
    for k in range(1, nb):
        send(emba.at[b], emba.at[b], p2s.at[k - 1], p2r.at[k - 1], (lax.rem(b + k, nb), s))
    for k in range(1, nb):
        await_ref(emba.at[lax.rem(b + nb - k, nb)], p2r.at[k - 1])

    doc_ids = lax.broadcasted_iota(jnp.int32, (nb, HD), 0)

    def fold(x):
        return x[:, 0:HD] + x[:, HD : 2 * HD] + x[:, 2 * HD : 3 * HD] + x[:, 3 * HD :]

    def dots(row):
        out = jnp.zeros((nb, HD), F32)
        for j in range(nb):
            prod = jnp.sum(fold(emba[j] * (emba[j] if row is None else row)), axis=0, keepdims=True)
            out = jnp.where(doc_ids == j, prod, out)
        return jnp.broadcast_to(jnp.sum(out, axis=1, keepdims=True), (nb, HD))

    posv = jnp.zeros((nb, HD), jnp.int32)
    for j in range(nb):
        posv = jnp.where(doc_ids == j, pos_ref[j], posv)
    rho = lax.rsqrt(dots(None) + EPS)

    def own_rho(row):
        total = jnp.sum(jnp.sum(fold(row * row), axis=0, keepdims=True), axis=1, keepdims=True)
        return jnp.broadcast_to(lax.rsqrt(total + EPS), (nb, HD))

    row_rho = own_rho(mine)
    sims = dots(mine) * rho * row_rho
    logits = 10.0 * sims - 2.0

    def pull(sign):
        return -10.0 / nb * sign / (1.0 + jnp.exp(sign * logits))

    pair = pull(jnp.where(doc_ids == pos_ref[b], 1.0, -1.0)) + pull(jnp.where(posv == b, 1.0, -1.0))
    pair = jnp.where(doc_ids == b, 0.0, pair) * (16.0 * ns * T)
    coef = pair * rho * row_rho
    self_coef = row_rho * row_rho * jnp.broadcast_to(jnp.sum(pair * sims, axis=0, keepdims=True), (nb, HD))
    grad = -self_coef[0:1, 0:1] * mine
    for j in range(nb):
        grad = grad + coef[j : j + 1, 0:1] * emba[j]
    gref[...] = grad / lenf

    total = jnp.zeros((T, HD), F32)
    for g in range(NY * H):
        x = sm[g] * (gref[g : g + 1, :] * gain_ref[0:1, g * GW : (g + 1) * GW])
        for j in range(G):
            total = total + x[:, j * HD : (j + 1) * HD]
    mean = jnp.sum(total, axis=1, keepdims=True) * (1.0 / (NY * H * GW))
    for g in range(NY * H):
        gained = gref[g : g + 1, :] * gain_ref[0:1, g * GW : (g + 1) * GW]
        out = jnp.where(valid_row, inv * (gained - sm[g] * mean), 0.0).astype(BF16)
        gro[g % H, g // H] = out
        lcopy(gro.at[g % H, g // H], out_gr.at[:, g * GW : (g + 1) * GW], gol.at[g]).start()
    for h in range(H):
        for k in (1, 3, 2):
            yy = yo(k)
            send(gro.at[h, yy], doi.at[h, y], grs.at[h, k - 1], grr.at[h, k - 1], ydev(yy))
        lcopy(gro.at[h, y], doi.at[h, y], grl.at[h]).start()

    def r1(h, way):
        dev, piece = (right, 0) if way == 0 else (left, 2)
        return rcopy(dkvo.at[h, 2, :, pl.ds(piece, 2)], rs1.at[h, way], r1s.at[h, way], r1r.at[h, way], dev)

    def r2(h, way):
        dev = right if way == 0 else left
        return rcopy(dkvo.at[h, 1 - way], rs2.at[h, way], r2s.at[h, way], r2r.at[h, way], dev)

    def gq_send(h, kk):
        yy = yo(kk)
        return rcopy(gqo.at[h, yy], out_gq.at[:, col(2 * y + h, GW)], gqs.at[h, kk - 1], gqr.at[h, kk - 1], ydev(yy))

    def gq_local(h):
        return lcopy(gqo.at[h, y], out_gq.at[:, col(2 * y + h, GW)], gql.at[h])

    def bwd_step(step, carry):
        rel = NZ - 1 - lax.div(step, H)
        h = lax.rem(step, H)

        @pl.when(rel == 3)
        def _():
            lcopy(gro.at[h, y], doi.at[h, y], grl.at[h]).wait()
            for k in range(1, NY):
                await_ref(doi.at[h, yo(NY - k)], grr.at[h, k - 1])

            def prep_g(yy, carry):
                for j in range(G):
                    dot_t[h, yy, :, j * T : (j + 1) * T] = doi[h, yy, :, j * HD : (j + 1) * HD].astype(F32).T
                dqa[h, yy] = jnp.zeros((HD, G * T), F32)
                return carry

            lax.fori_loop(0, NY, prep_g, 0)

        dka[...] = jnp.zeros((BK, HD), F32)
        dva[...] = jnp.zeros((BK, HD), F32)

        def chunk(t, carry):
            kk = lax.rem(t + 1, NY)
            yy = yo(kk)
            vals = kvb[h, rel, 1].reshape(BK, HD)
            half = G * T // 2
            for part in range(2):
                lanes = slice(part * half, (part + 1) * half)
                r = jnp.exp2((mb[h, rel, yy, :, lanes] - mrun[h, yy, :, lanes]) * LOG2E_FACTOR) * linv[h, yy, :, lanes]
                do = (dot_t[h, yy, :, lanes] * r).astype(BF16)
                delta = jnp.sum(do.astype(F32) * acc[h, yy, 0:HD, lanes], axis=0, keepdims=True)
                e = est[h, rel, yy, :, lanes]
                dp = dot(vals, do)
                ds = (e.astype(F32) * (dp - delta)).astype(BF16)
                dva[...] += dot(e, do, ((1,), (1,)))
                dka[...] += dot(ds, qs[h, yy, lanes, :])
                dqa[h, yy, :, lanes] += dot(kzt[h, rel], ds)

            @pl.when(rel == 0)
            def _():
                for j in range(G):
                    part = dqa[h, yy, :, j * T : (j + 1) * T] * FACTOR
                    gqo[h, yy, :, j * HD : (j + 1) * HD] = part.T.astype(BF16)

                @pl.when(kk > 0)
                def _():
                    gq_send(h, kk).start()

                @pl.when(kk == 0)
                def _():
                    gq_local(h).start()

            return carry

        lax.fori_loop(0, NY, chunk, 0)

        def store(slot, added):
            for c, ref in ((0, dka), (1, dva)):
                for p in range(NY):
                    x = ref[p * T : (p + 1) * T, :]
                    if c == 0:
                        x = x * FACTOR
                    if added is not None and p // 2 == added:
                        x = x + rs1[h, added, c, p % 2].astype(F32)
                    dkvo[h, slot, c, p] = x.astype(BF16)

        @pl.when(rel == 3)
        def _():
            store(2, None)
            r1(h, 0).start()
            r1(h, 1).start()

        @pl.when(rel == 2)
        def _():
            await_ref(rs1.at[h, 0], r1r.at[h, 0])
            store(1, 0)
            r2(h, 0).start()

        @pl.when(rel == 1)
        def _():
            await_ref(rs1.at[h, 1], r1r.at[h, 1])
            store(0, 1)
            r2(h, 1).start()

        @pl.when(rel == 0)
        def _():
            own[h, 0] = dka[...] * FACTOR
            own[h, 1] = dva[...]

        return carry

    lax.fori_loop(0, NZ * H, bwd_step, 0)

    def loss_row(i, total):
        row = emba[i]
        logit = 10.0 * (dots(row) * rho * own_rho(row)) - 2.0
        x = jnp.where(doc_ids == pos_ref[i], -logit, logit)
        term = jnp.maximum(x, 0.0) + jnp.log(1.0 + jnp.exp(-jnp.abs(x)))
        return total + jnp.where(doc_ids == i, 0.0, term)

    terms = lax.fori_loop(0, nb, loss_row, jnp.zeros((nb, HD), F32))
    loss_ref[0, 0] = jnp.sum(terms) * (1.0 / (HD * nb))

    for h in range(H):
        await_ref(rs2.at[h, 0], r2r.at[h, 0])
        await_ref(rs2.at[h, 1], r2r.at[h, 1])
        for p in range(NY):
            valid = lax.broadcasted_iota(jnp.int32, (T, HD), 0) + (p * NZ + zh) * T < length
            for c in range(2):
                x = own[h, c, p * T : (p + 1) * T, :] + rs2[h, 0, c, p].astype(F32) + rs2[h, 1, c, p].astype(F32)
                fin[h, c, p] = jnp.where(valid, x, 0.0).astype(BF16)
        for c, out in ((0, out_gk), (1, out_gv)):
            for k in (1, 3, 2):
                yy = yo(k)
                send(fin.at[h, c, yy], out.at[:, col(2 * y + h, HD)], gks.at[h, c, k - 1], gkr.at[h, c, k - 1], ydev(yy))
            lcopy(fin.at[h, c, y], out.at[:, col(2 * y + h, HD)], gkl.at[h, c]).start()

    for g in range(NY * H):
        lcopy(gro.at[g % H, g // H], out_gr.at[:, g * GW : (g + 1) * GW], gol.at[g]).wait()
    for h in range(H):
        gq_local(h).wait()
        for k in range(1, NY):
            await_ref(out_gq.at[:, col(2 * yo(NY - k) + h, GW)], gqr.at[h, k - 1])
        for c, out in ((0, out_gk), (1, out_gv)):
            lcopy(fin.at[h, c, y], out.at[:, col(2 * y + h, HD)], gkl.at[h, c]).wait()
            for k in range(1, NY):
                await_ref(out.at[:, col(2 * yo(NY - k) + h, HD)], gkr.at[h, c, k - 1])
    for copy in sends:
        copy.wait_send()
    for h in range(H):
        for way in range(2):
            hop2(h, way).wait_send()
            r1(h, way).wait_send()
            r2(h, way).wait_send()
        for k in range(1, NY):
            att_send(h, k).wait_send()
            gq_send(h, k).wait_send()


def on_device(nb, residual, query_proj, key_proj, value_proj, norm_gain, lengths, positives):
    T, D = residual.shape
    ns = NY * NZ
    BK, QC = NY * T, G * T
    V = pltpu.VMEM
    S = pltpu.SemaphoreType.DMA
    scratch = [
        V((H, NZ, 2, NY, T, HD), BF16),
        V((H, NZ, BK, HD), BF16),
        V((H, NZ, HD, BK), BF16),
        V((H, NZ, HD + 16, BK), BF16),
        V((H, NY, T, GW), BF16),
        V((H, NY, QC, HD), BF16),
        V((H, NY, HD, QC), BF16),
        V((H, NZ, NY, BK, QC), BF16),
        V((H, NZ, NY, 1, QC), F32),
        V((H, NY, 1, QC), F32),
        V((H, NY, 1, QC), F32),
        V((H, NY, HD + 16, QC), F32),
        V((H, NY, T, GW), BF16),
        V((H, NY, T, GW), BF16),
        V((T, D), BF16),
        V((NY * H, T, GW), F32),
        V((NY * H, GW), F32),
        V((ns, NY * H, GW), F32),
        V((nb, NY * H, GW), F32),
        V((NY * H, GW), F32),
        V((H, NY, T, GW), BF16),
        V((H, NY, T, GW), BF16),
        V((H, NY, HD, QC), F32),
        V((H, NY, HD, QC), F32),
        V((H, NY, T, GW), BF16),
        V((BK, HD), F32),
        V((BK, HD), F32),
        V((H, 3, 2, NY, T, HD), BF16),
        V((H, 2, BK, HD), F32),
        V((H, 2, 2, 2, T, HD), BF16),
        V((H, 2, 2, NY, T, HD), BF16),
        V((H, 2, NY, T, HD), BF16),
        S((H, 2, NY - 1)), S((H, 2, NY - 1)), S((H, 2)),
        S((H, NY - 1)), S((H, NY - 1)), S((H,)),
        S((H, 2, NY)), S((H, 2, NY)), S((H, 2)), S((H, 2)),
        S((H, NY - 1)), S((H, NY - 1)), S((H,)), S,
        S((ns - 1,)), S((ns - 1,)), S((nb - 1,)), S((nb - 1,)),
        S((H, NY - 1)), S((H, NY - 1)), S((H,)), S((NY * H,)),
        S((H, 2)), S((H, 2)), S((H, 2)), S((H, 2)),
        S((H, NY - 1)), S((H, NY - 1)), S((H,)),
        S((H, 2, NY - 1)), S((H, 2, NY - 1)), S((H, 2)),
    ]
    any_spec = pl.BlockSpec(memory_space=pl.ANY)
    smem = pl.BlockSpec(memory_space=pltpu.SMEM)
    loss, gr, gq, gk, gv = pl.pallas_call(
        functools.partial(kernel, nb, T),
        out_shape=(
            jax.ShapeDtypeStruct((1, 1), F32),
            jax.ShapeDtypeStruct((T, D), BF16),
            jax.ShapeDtypeStruct((T, D), BF16),
            jax.ShapeDtypeStruct(key_proj.shape, BF16),
            jax.ShapeDtypeStruct(key_proj.shape, BF16),
        ),
        in_specs=[smem, smem, any_spec, any_spec, any_spec, any_spec, pl.BlockSpec(memory_space=pltpu.VMEM)],
        out_specs=(smem, any_spec, any_spec, any_spec, any_spec),
        scratch_shapes=scratch,
        compiler_params=pltpu.CompilerParams(
            collective_id=0, has_side_effects=True, vmem_limit_bytes=56 * 1024 * 1024
        ),
        cost_estimate=pl.CostEstimate(flops=13 * 10**9, bytes_accessed=6 * 2**20, transcendentals=2**23),
        name="attention_backward",
    )(lengths, positives, residual, query_proj, key_proj, value_proj, norm_gain.reshape(1, D))
    return loss.reshape(()), gr, gq, gk, gv


def solution(mesh):
    rows = P(("batch", "seq"), None)
    return jax.shard_map(
        functools.partial(on_device, mesh.shape["batch"]),
        mesh=mesh,
        in_specs=(rows, rows, rows, rows, P(), P("batch"), P()),
        out_specs=(P(), rows, rows, rows, rows),
        check_vma=False,
    )
```

time: 631 us -> 156 us (0.25)
  the two profiles are of different devices: /device:TPU:8 before, /device:TPU:26 now
where the time goes in v1:
time: 156 us
  Pallas kernels  148 us (95%)
  local copies, waits for them, and re-layouts  5.22 us (3%)
  between operations  3.12 us (2%)
    pallas_call x1, Pallas kernels, on_device(): pl.pallas_call(functools.partial(kernel, nb, T), out_shape=(jax.ShapeDtyp...  148 us
    unnamed x10, local copies, waits for them, and re-layouts  5.22 us

profile of v1, /device:TPU:26, one launch (start us, length us, event | category | flops | bytes accessed | tf_op | source)
XLA Modules:
  0.0 156.0 jit_solution(14830877435483573768)
XLA Ops:
  1.3 147.7 %attention_backward.1 = (f32[1,1]{1,0:T(1,128)}, bf16[128,4096]{1,0:T(8,128)(2,1)}, bf16[128,4096]{1,0:T(8,128)(2,1)}, bf16[128,1024]{1,0:T(8,128)(2,1)}, bf16[128,1024]{1,0:T(8,128)(2,1)}) custom-call(s32[1]{0:T(128)S(6)} %copy.17.len_ref, s32[16]{0:T(128)} %pos_ref.1, bf16[128,4096]{1,0:T(8,128)(2,1)} %res_hbm.1, bf16[128,4096]{1,0:T(8,128)(2,1)} %q_hbm.1, ...), custom_call_target="tpu_custom_call" | custom-call | flops 12999999488 | bytes 6291456 | tf_op jit(solution)/shard_map/attention_backward/pallas_call | solution.py:515
  149.7 0.0 copy-start
  149.7 2.4 %copy.19 = bf16[128,4096]{1,0:T(8,128)(2,1)} copy(bf16[128,4096]{1,0:T(8,128)(2,1)} %get-tuple-element.21) | data formatting | bytes 2097152
  152.1 0.0 copy-done
  152.1 0.0 copy-start.2
  152.1 1.0 copy.20
  153.1 0.1 copy-done.2
  153.2 0.0 copy-start.1
  153.2 0.7 copy.21
  153.9 0.3 copy-done.1
  154.2 0.7 copy.22
Async XLA Ops:
  149.7 2.4 %copy-start = (bf16[128,4096]{1,0:T(8,128)(2,1)S(1)}, bf16[128,4096]{1,0:T(8,128)(2,1)}, u32[]{:S(2)}) copy-start(bf16[128,4096]{1,0:T(8,128)(2,1)} %get-tuple-element.22) | copy-start | bytes 3145732
  152.1 1.1 copy-start.2
  153.2 1.0 copy-start.1

commit v2 on v1

v2 whole, which is shorter than its diff:
```python
import functools
import math

import jax
import jax.numpy as jnp
from jax import lax
from jax.experimental import pallas as pl
from jax.experimental.pallas import tpu as pltpu
from jax.sharding import PartitionSpec as P

MESH = pl.DeviceIdType.MESH
HD = 128
NY = 4
NZ = 4
H = 2
G = 4
GW = G * HD
EPS = 1e-6
F32 = jnp.float32
BF16 = jnp.bfloat16
FACTOR = 1.0 / math.sqrt(HD)
LOG2E_FACTOR = FACTOR * math.log2(math.e)


def dot(a, b, dims=((1,), (0,))):
    return lax.dot_general(a, b, (dims, ((), ())), preferred_element_type=F32)


def kernel(
    nb, t_rows,
    len_ref, pos_ref, res_hbm, q_hbm, k_hbm, v_hbm, gain_ref,
    loss_ref, out_gr, out_gq, out_gk, out_gv,
    kvb, kfx, kzt, vta, qin, qs, qt, est, mb, mrun, linv, acc, rin, smt,
    rsq, rsa, invr, pz, pza, emba, sga, lra, gbt, mrw, msa, mrc, dot_t, gro, dqa, gqo, dka, dva, dkvo, own, rs1, rs2, fin,
    kvs, kvr, kvl, qss, qsr, qsl, rns, rnr, rnl, z1s, z1r, z2s, z2r,
    sqs, sqr, pzs, pzr, ems, emr, sis, sir, los, lor, mns, mnr,
    grs, grr, grl, r1s, r1r, r2s, r2r, gqs, gqr, gql, gks, gkr, gkl,
):
    T = t_rows
    BK = NY * T
    NG = H * G
    b = lax.axis_index("batch")
    s = lax.axis_index("seq")
    y = lax.div(s, NZ)
    zh = lax.rem(s, NZ)
    right = (b, y * NZ + lax.rem(zh + 1, NZ))
    left = (b, y * NZ + lax.rem(zh + NZ - 1, NZ))

    def yo(k):
        return lax.rem(y + k, NY)

    def zo(k):
        return lax.rem(zh + k, NZ)

    def bo(k):
        return lax.rem(b + k, nb)

    def ydev(yy):
        return (b, yy * NZ + zh)

    def zdev(zz):
        return (b, y * NZ + zz)

    def col(index, width):
        return pl.ds(pl.multiple_of(index * width, width), width)

    def rcopy(src, dst, ssem, rsem, dev):
        return pltpu.make_async_remote_copy(
            src_ref=src, dst_ref=dst, send_sem=ssem, recv_sem=rsem, device_id=dev, device_id_type=MESH
        )

    def lcopy(src, dst, sem):
        return pltpu.make_async_copy(src, dst, sem)

    def await_ref(ref, sem):
        pltpu.make_async_copy(ref, ref, sem).wait()

    sends = []

    def send(src, dst, ssem, rsem, dev):
        copy = rcopy(src, dst, ssem, rsem, dev)
        copy.start()
        sends.append(copy)

    length = len_ref[0]
    lenf = length.astype(F32)

    for h in range(H):
        for c, src in ((0, k_hbm), (1, v_hbm)):
            lcopy(src.at[:, col(2 * y + h, HD)], kvb.at[h, 0, c, y], kvl.at[h, c]).start()
        lcopy(q_hbm.at[:, col(2 * y + h, GW)], qin.at[h, y], qsl.at[h]).start()
        lcopy(res_hbm.at[:, col(2 * y + h, GW)], rin.at[h, y], rnl.at[h]).start()

    barrier = pltpu.get_barrier_semaphore()
    for k in range(1, NY):
        pl.semaphore_signal(barrier, inc=1, device_id=ydev(yo(k)), device_id_type=MESH)
    for k in range(1, NZ):
        pl.semaphore_signal(barrier, inc=1, device_id=zdev(zo(k)), device_id_type=MESH)
    for k in range(1, nb):
        pl.semaphore_signal(barrier, inc=1, device_id=(bo(k), s), device_id_type=MESH)
    pl.semaphore_wait(barrier, NY - 1 + NZ - 1 + nb - 1)

    for h in range(H):
        for k in (1, 3, 2):
            yy = yo(k)
            for c, src in ((0, k_hbm), (1, v_hbm)):
                send(src.at[:, col(2 * yy + h, HD)], kvb.at[h, 0, c, y], kvs.at[h, c, k - 1], kvr.at[h, c, k - 1], ydev(yy))
        for k in (1, 3, 2):
            yy = yo(k)
            send(q_hbm.at[:, col(2 * yy + h, GW)], qin.at[h, y], qss.at[h, k - 1], qsr.at[h, k - 1], ydev(yy))
    for h in range(H):
        for k in (1, 3, 2):
            yy = yo(k)
            send(res_hbm.at[:, col(2 * yy + h, GW)], rin.at[h, y], rns.at[h, k - 1], rnr.at[h, k - 1], ydev(yy))

    for h in range(H):
        for k in (0, 1, 3, 2):
            p = yo(NY - k)
            for c, src in ((0, k_hbm), (1, v_hbm)):
                if k == 0:
                    lcopy(src.at[:, col(2 * y + h, HD)], kvb.at[h, 0, c, y], kvl.at[h, c]).wait()
                else:
                    await_ref(kvb.at[h, 0, c, p], kvr.at[h, c, k - 1])
            send(kvb.at[h, 0, :, p], kvb.at[h, 1, :, p], z1s.at[h, 0, k], z1r.at[h, 0, k], right)
            send(kvb.at[h, 0, :, p], kvb.at[h, 2, :, p], z1s.at[h, 1, k], z1r.at[h, 1, k], left)

    def hop2(h, way):
        src, dev, piece = (1, right, 0) if way == 0 else (2, left, 2)
        return rcopy(
            kvb.at[h, src, :, pl.ds(piece, 2)], kvb.at[h, 3, :, pl.ds(piece, 2)], z2s.at[h, way], z2r.at[h, way], dev
        )

    def forward_hops(h):
        for way in range(2):
            for k in range(NY):
                await_ref(kvb.at[h, 1 + way, :, yo(NY - k)], z1r.at[h, way, k])
            hop2(h, way).start()

    def await_columns(h, src, dst, lsem, rsem):
        lcopy(src.at[:, col(2 * y + h, GW)], dst.at[h, y], lsem.at[h]).wait()
        for k in range(1, NY):
            await_ref(dst.at[h, yo(NY - k)], rsem.at[h, k - 1])

    def prep_q(h):
        def body(yy, carry):
            for j in range(G):
                head = qin[h, yy, :, j * HD : (j + 1) * HD]
                qs[h, yy, j * T : (j + 1) * T, :] = head
                qt[h, yy, :, j * T : (j + 1) * T] = head.astype(F32).T.astype(BF16)
            mrun[h, yy] = jnp.full((1, G * T), -3e38, F32)
            acc[h, yy] = jnp.zeros((HD + 16, G * T), F32)
            return carry

        lax.fori_loop(0, NY, body, 0)

    def prep_res(h):
        def body(yy, carry):
            for j in range(G):
                smt[h, yy, :, j * T : (j + 1) * T] = rin[h, yy, :, j * HD : (j + 1) * HD].astype(F32).T
            return carry

        lax.fori_loop(0, NY, body, 0)

    def prep_kv(h, rel, zb):
        first_key = kvb[h, rel, 0, 0, 0:1, :].astype(F32)
        for yy in range(NY):
            base = (yy * NZ + zb) * T
            valid = lax.broadcasted_iota(jnp.int32, (T, HD), 0) + base < length
            rows = slice(yy * T, (yy + 1) * T)
            kp = kvb[h, rel, 0, yy].astype(F32)
            vp = kvb[h, rel, 1, yy].astype(F32)
            kfx[h, rel, rows, :] = jnp.where(valid, kp, first_key).astype(BF16)
            kzt[h, rel, :, rows] = jnp.where(valid, kp, 0.0).T.astype(BF16)
            vta[h, rel, 0:HD, rows] = jnp.where(valid, vp, 0.0).T.astype(BF16)
            lanes = lax.broadcasted_iota(jnp.int32, (16, T), 1) + base < length
            vta[h, rel, HD : HD + 16, rows] = jnp.where(lanes, 1.0, 0.0).astype(BF16)

    halves = [slice(part * (G * T // 2), (part + 1) * (G * T // 2)) for part in range(2)]

    def attend(h, rel, yy):
        for lanes in halves:
            sc = dot(kfx[h, rel], qt[h, yy, :, lanes])
            m = jnp.max(sc, axis=0, keepdims=True)
            e = jnp.exp2((sc - m) * LOG2E_FACTOR).astype(BF16)
            est[h, rel, yy, :, lanes] = e
            mb[h, rel, yy, :, lanes] = m
            o = dot(vta[h, rel], e)
            mo = mrun[h, yy, :, lanes]
            mn = jnp.maximum(mo, m)
            keep = jnp.exp2((mo - mn) * LOG2E_FACTOR)
            add = jnp.exp2((m - mn) * LOG2E_FACTOR)
            acc[h, yy, :, lanes] = acc[h, yy, :, lanes] * keep + o * add
            mrun[h, yy, :, lanes] = mn

    def over_chunks(body):
        def step(yy, carry):
            body(yy)
            return carry

        lax.fori_loop(0, NY, step, 0)

    def own_step(h, carry):
        @pl.when(h == 1)
        def _():
            forward_hops(0)

        await_columns(h, q_hbm, qin, qsl, qsr)
        prep_q(h)
        prep_kv(h, 0, zh)
        over_chunks(lambda yy: attend(h, 0, yy))
        return carry

    def near_step(m, carry):
        h = lax.div(m, 2)
        rel = 1 + lax.rem(m, 2)

        @pl.when(m == 2)
        def _():
            forward_hops(1)

        prep_kv(h, rel, zo(5 - 2 * rel))
        over_chunks(lambda yy: attend(h, rel, yy))
        return carry

    def far_step(h, carry):
        await_columns(h, res_hbm, rin, rnl, rnr)
        prep_res(h)
        for way in range(2):
            await_ref(kvb.at[h, 3, :, pl.ds(2 * way, 2)], z2r.at[h, way])
        prep_kv(h, 3, zo(2))

        def chunk(yy):
            attend(h, 3, yy)
            li = 1.0 / acc[h, yy, HD : HD + 1, :]
            linv[h, yy] = li
            o = acc[h, yy, 0:HD, :] * li
            acc[h, yy, 0:HD, :] = o
            x = smt[h, yy] + o.astype(BF16).astype(F32)
            smt[h, yy] = x
            sq = jnp.sum(x * x, axis=0, keepdims=True)
            rsq[yy] = rsq[yy] + sum(sq[:, j * T : (j + 1) * T] for j in range(G))

        over_chunks(chunk)
        return carry

    rsq[...] = jnp.zeros((NY, 1, T), F32)
    lax.fori_loop(0, H, own_step, 0)
    lax.fori_loop(0, 2 * H, near_step, 0)
    lax.fori_loop(0, H, far_step, 0)

    def sum_along_y(src, gathered, ssem, rsem):
        for k in (2, 1, 3):
            send(src, gathered.at[y], ssem.at[k - 1], rsem.at[k - 1], ydev(yo(k)))
        gathered[y] = src[...]
        for k in (1, 3, 2):
            await_ref(gathered.at[yo(NY - k)], rsem.at[k - 1])
        return (gathered[0] + gathered[1]) + (gathered[2] + gathered[3])

    mean_square = sum_along_y(rsq, rsa, sqs, sqr) * (1.0 / (NY * NG * HD))
    inv = lax.rsqrt(mean_square + EPS)
    lane = lax.broadcasted_iota(jnp.int32, (NY, 1, T), 2)
    chunk_id = lax.broadcasted_iota(jnp.int32, (NY, 1, T), 0)
    live = (chunk_id * NZ + zh) * T + lane < length
    inv = jnp.where(live, inv, 0.0)
    invr[...] = inv

    for h in range(H):
        for j in range(G):
            part = smt[h, 0, :, j * T : (j + 1) * T] * inv[0]
            for yy in range(1, NY):
                part = part + smt[h, yy, :, j * T : (j + 1) * T] * inv[yy]
            pz[h * G + j : h * G + j + 1, :] = jnp.sum(part.T, axis=0, keepdims=True)
    gain = gain_ref[y]
    pz[...] = pz[...] * gain / lenf
    for k in (2, 1, 3):
        send(pz, pza.at[zh], pzs.at[k - 1], pzr.at[k - 1], zdev(zo(k)))
    pza[zh] = pz[...]
    for k in (1, 3, 2):
        await_ref(pza.at[zo(NZ - k)], pzr.at[k - 1])
    mine = (pza[0] + pza[1]) + (pza[2] + pza[3])
    emba[b] = mine
    for k in range(1, nb):
        send(emba.at[b], emba.at[b], ems.at[k - 1], emr.at[k - 1], (bo(k), s))
    for k in range(1, nb):
        await_ref(emba.at[bo(nb - k)], emr.at[k - 1])

    doc_ids = lax.broadcasted_iota(jnp.int32, (nb, HD), 0)
    lane_ids = lax.broadcasted_iota(jnp.int32, (nb, HD), 1)
    dots = jnp.zeros((nb, HD), F32)
    squares = jnp.zeros((nb, HD), F32)
    for j in range(nb):
        row = emba[j]
        dots = jnp.where(doc_ids == j, jnp.sum(row * mine, axis=0, keepdims=True), dots)
        squares = jnp.where(doc_ids == j, jnp.sum(row * row, axis=0, keepdims=True), squares)
    dots = jnp.broadcast_to(jnp.sum(dots, axis=1, keepdims=True), (nb, HD))
    squares = jnp.broadcast_to(jnp.sum(squares, axis=1, keepdims=True), (nb, HD))
    sga[NY] = jnp.where(lane_ids < HD // 2, dots, squares)
    both = sum_along_y(sga.at[NY], sga, sis, sir)
    dots = jnp.broadcast_to(both[:, 0:1], (nb, HD))
    rho = lax.rsqrt(jnp.broadcast_to(both[:, HD // 2 : HD // 2 + 1], (nb, HD)) + EPS)
    row_rho = jnp.broadcast_to(jnp.sum(jnp.where(doc_ids == b, rho, 0.0), axis=0, keepdims=True), (nb, HD))
    sims = dots * rho * row_rho
    logits = 10.0 * sims - 2.0
    posv = jnp.zeros((nb, HD), jnp.int32)
    for j in range(nb):
        posv = jnp.where(doc_ids == j, pos_ref[j], posv)
    sign = jnp.where(doc_ids == pos_ref[b], 1.0, -1.0)

    def pull(label):
        return -10.0 / nb * label / (1.0 + jnp.exp(label * logits))

    pair = pull(sign) + pull(jnp.where(posv == b, 1.0, -1.0))
    pair = jnp.where(doc_ids == b, 0.0, pair) * (16.0 * NY * NZ * T)
    coef = pair * rho * row_rho
    self_coef = row_rho * row_rho * jnp.broadcast_to(jnp.sum(pair * sims, axis=0, keepdims=True), (nb, HD))
    grad = -self_coef[0:1, :] * mine
    for j in range(nb):
        grad = grad + coef[j : j + 1, :] * emba[j]
    gained = grad / lenf * gain

    for i in range(NG):
        gbt[i] = jnp.broadcast_to(gained[i : i + 1, :], (T, HD)).T
    for yy in range(NY):
        part = gbt[0] * smt[0, yy, :, 0:T]
        for i in range(1, NG):
            j = i % G
            part = part + gbt[i] * smt[i // G, yy, :, j * T : (j + 1) * T]
        mrw[yy] = jnp.sum(part, axis=0, keepdims=True)
    mean = sum_along_y(mrw, msa, mns, mnr) * invr[...] * (1.0 / (NY * NG * HD))
    mrw_scale = invr[...] * invr[...] * mean

    def r1(h, way):
        dev, piece = (right, 0) if way == 0 else (left, 2)
        return rcopy(dkvo.at[h, 2, :, pl.ds(piece, 2)], rs1.at[h, way], r1s.at[h, way], r1r.at[h, way], dev)

    def r2(h, way):
        dev = right if way == 0 else left
        return rcopy(dkvo.at[h, 1 - way], rs2.at[h, way], r2s.at[h, way], r2r.at[h, way], dev)

    def gq_send(h, kk):
        yy = yo(kk)
        return rcopy(gqo.at[h, yy], out_gq.at[:, col(2 * y + h, GW)], gqs.at[h, kk - 1], gqr.at[h, kk - 1], ydev(yy))

    def gq_local(h):
        return lcopy(gqo.at[h, y], out_gq.at[:, col(2 * y + h, GW)], gql.at[h])

    def gr_send(h, kk):
        yy = yo(kk)
        return rcopy(gro.at[h, yy], out_gr.at[:, col(2 * y + h, GW)], grs.at[h, kk - 1], grr.at[h, kk - 1], ydev(yy))

    def gr_local(h):
        return lcopy(gro.at[h, y], out_gr.at[:, col(2 * y + h, GW)], grl.at[h])

    def pull_back(h, rel, yy):
        vals = kvb[h, rel, 1].reshape(BK, HD)
        for lanes in halves:
            r = jnp.exp2((mb[h, rel, yy, :, lanes] - mrun[h, yy, :, lanes]) * LOG2E_FACTOR) * linv[h, yy, :, lanes]
            do = (dot_t[h, yy, :, lanes].astype(F32) * r).astype(BF16)
            delta = jnp.sum(do.astype(F32) * acc[h, yy, 0:HD, lanes], axis=0, keepdims=True)
            e = est[h, rel, yy, :, lanes]
            dp = dot(vals, do)
            ds = (e.astype(F32) * (dp - delta)).astype(BF16)
            dva[...] += dot(e, do, ((1,), (1,)))
            dka[...] += dot(ds, qs[h, yy, lanes, :])
            dqa[h, yy, :, lanes] += dot(kzt[h, rel], ds)

    def clear():
        dka[...] = jnp.zeros((BK, HD), F32)
        dva[...] = jnp.zeros((BK, HD), F32)

    def store(h, slot, added):
        for c, ref in ((0, dka), (1, dva)):
            for p in range(NY):
                x = ref[p * T : (p + 1) * T, :]
                if c == 0:
                    x = x * FACTOR
                if added is not None and p // 2 == added:
                    x = x + rs1[h, added, c, p % 2].astype(F32)
                dkvo[h, slot, c, p] = x.astype(BF16)

    def far_back(h, carry):
        for yy in range(NY):
            a = jnp.concatenate([invr[yy]] * G, axis=1)
            c = jnp.concatenate([mrc[yy]] * G, axis=1)
            g = jnp.concatenate([gbt[h * G + j] for j in range(G)], axis=1)
            dot_t[h, yy] = (g * a - smt[h, yy] * c).astype(BF16)
            dqa[h, yy] = jnp.zeros((HD, G * T), F32)
        clear()
        over_chunks(lambda yy: pull_back(h, 3, yy))
        store(h, 2, None)
        r1(h, 0).start()
        r1(h, 1).start()

        def give(t, carry):
            kk = lax.rem(t + 1, NY)
            yy = yo(kk)
            for j in range(G):
                gro[h, yy, :, j * HD : (j + 1) * HD] = dot_t[h, yy, :, j * T : (j + 1) * T].astype(F32).T.astype(BF16)

            @pl.when(kk > 0)
            def _():
                gr_send(h, kk).start()

            @pl.when(kk == 0)
            def _():
                gr_local(h).start()

            return carry

        lax.fori_loop(0, NY, give, 0)
        return carry

    def near_back(m, carry):
        h = lax.div(m, 2)
        way = lax.rem(m, 2)
        rel = 2 - way
        clear()
        over_chunks(lambda yy: pull_back(h, rel, yy))
        for w in range(2):

            @pl.when(way == w)
            def _(w=w):
                await_ref(rs1.at[h, w], r1r.at[h, w])
                store(h, 1 - w, w)
                r2(h, w).start()

        return carry

    def own_back(h, carry):
        clear()

        def chunk(t, carry):
            kk = lax.rem(t + 1, NY)
            yy = yo(kk)
            pull_back(h, 0, yy)
            for j in range(G):
                part = dqa[h, yy, :, j * T : (j + 1) * T] * FACTOR
                gqo[h, yy, :, j * HD : (j + 1) * HD] = part.T.astype(BF16)

            @pl.when(kk > 0)
            def _():
                gq_send(h, kk).start()

            @pl.when(kk == 0)
            def _():
                gq_local(h).start()

            return carry

        lax.fori_loop(0, NY, chunk, 0)
        own[h, 0] = dka[...] * FACTOR
        own[h, 1] = dva[...]
        return carry

    mrc[...] = mrw_scale
    lax.fori_loop(0, H, far_back, 0)

    x = -sign * logits
    term = jnp.maximum(x, 0.0) + jnp.log(1.0 + jnp.exp(-jnp.abs(x)))
    term = jnp.sum(jnp.where(doc_ids == b, 0.0, term), axis=0, keepdims=True)
    lra[b] = jnp.broadcast_to(term, (8, HD))
    for k in range(1, nb):
        send(lra.at[b], lra.at[b], los.at[k - 1], lor.at[k - 1], (bo(k), s))

    lax.fori_loop(0, 2 * H, near_back, 0)
    lax.fori_loop(0, H, own_back, 0)

    for k in range(1, nb):
        await_ref(lra.at[bo(nb - k)], lor.at[k - 1])
    loss = lra[0]
    for j in range(1, nb):
        loss = loss + lra[j]
    loss_ref[0, 0] = jnp.sum(loss) * (1.0 / (8 * HD * nb))

    for h in range(H):
        await_ref(rs2.at[h, 0], r2r.at[h, 0])
        await_ref(rs2.at[h, 1], r2r.at[h, 1])
        for p in range(NY):
            valid = lax.broadcasted_iota(jnp.int32, (T, HD), 0) + (p * NZ + zh) * T < length
            for c in range(2):
                x = own[h, c, p * T : (p + 1) * T, :] + rs2[h, 0, c, p].astype(F32) + rs2[h, 1, c, p].astype(F32)
                fin[h, c, p] = jnp.where(valid, x, 0.0).astype(BF16)
        for c, out in ((0, out_gk), (1, out_gv)):
            for k in (2, 1, 3):
                yy = yo(k)
                send(fin.at[h, c, yy], out.at[:, col(2 * y + h, HD)], gks.at[h, c, k - 1], gkr.at[h, c, k - 1], ydev(yy))
            lcopy(fin.at[h, c, y], out.at[:, col(2 * y + h, HD)], gkl.at[h, c]).start()

    for h in range(H):
        gq_local(h).wait()
        gr_local(h).wait()
        for k in range(1, NY):
            await_ref(out_gr.at[:, col(2 * yo(NY - k) + h, GW)], grr.at[h, k - 1])
            await_ref(out_gq.at[:, col(2 * yo(NY - k) + h, GW)], gqr.at[h, k - 1])
        for c, out in ((0, out_gk), (1, out_gv)):
            lcopy(fin.at[h, c, y], out.at[:, col(2 * y + h, HD)], gkl.at[h, c]).wait()
            for k in range(1, NY):
                await_ref(out.at[:, col(2 * yo(NY - k) + h, HD)], gkr.at[h, c, k - 1])
    for copy in sends:
        copy.wait_send()
    for h in range(H):
        for way in range(2):
            hop2(h, way).wait_send()
            r1(h, way).wait_send()
            r2(h, way).wait_send()
        for k in range(1, NY):
            gr_send(h, k).wait_send()
            gq_send(h, k).wait_send()


def copy_kernel(parts, *refs):
    n = len(refs) // 2
    sems = refs[-1]
    copies = []
    for i in range(n):
        src, dst = refs[i], refs[n + i]
        rows = src.shape[0] // parts
        for p in range(parts):
            span = pl.ds(p * rows, rows)
            copies.append(pltpu.make_async_copy(src.at[span], dst.at[span], sems.at[i, p]))
    for copy in copies:
        copy.start()
    for copy in copies:
        copy.wait()


def own_buffers(arrays):
    parts = 4
    any_spec = pl.BlockSpec(memory_space=pl.ANY)
    return pl.pallas_call(
        functools.partial(copy_kernel, parts),
        out_shape=tuple(jax.ShapeDtypeStruct(x.shape, x.dtype) for x in arrays),
        in_specs=[any_spec] * len(arrays),
        out_specs=(any_spec,) * len(arrays),
        scratch_shapes=[pltpu.SemaphoreType.DMA((len(arrays), parts))],
        compiler_params=pltpu.CompilerParams(vmem_limit_bytes=56 * 1024 * 1024),
        cost_estimate=pl.CostEstimate(flops=0, bytes_accessed=5 * 2**20, transcendentals=0),
        name="copy_out",
    )(*arrays)


def on_device(nb, residual, query_proj, key_proj, value_proj, norm_gain, lengths, positives):
    T, D = residual.shape
    BK, QC, NG = NY * T, G * T, H * G
    V = pltpu.VMEM
    S = pltpu.SemaphoreType.DMA
    columns = V((H, NY, T, GW), BF16)
    scratch = [
        V((H, NZ, 2, NY, T, HD), BF16),
        V((H, NZ, BK, HD), BF16),
        V((H, NZ, HD, BK), BF16),
        V((H, NZ, HD + 16, BK), BF16),
        columns,
        V((H, NY, QC, HD), BF16),
        V((H, NY, HD, QC), BF16),
        V((H, NZ, NY, BK, QC), BF16),
        V((H, NZ, NY, 1, QC), F32),
        V((H, NY, 1, QC), F32),
        V((H, NY, 1, QC), F32),
        V((H, NY, HD + 16, QC), F32),
        columns,
        V((H, NY, HD, QC), F32),
        V((NY, 1, T), F32), V((NY, NY, 1, T), F32), V((NY, 1, T), F32),
        V((NG, HD), F32), V((NZ, NG, HD), F32),
        V((nb, NG, HD), F32),
        V((NY + 1, nb, HD), F32),
        V((nb, 8, HD), F32),
        V((NG, HD, T), F32),
        V((NY, 1, T), F32), V((NY, NY, 1, T), F32), V((NY, 1, T), F32),
        V((H, NY, HD, QC), BF16),
        columns,
        V((H, NY, HD, QC), F32),
        columns,
        V((BK, HD), F32),
        V((BK, HD), F32),
        V((H, 3, 2, NY, T, HD), BF16),
        V((H, 2, BK, HD), F32),
        V((H, 2, 2, 2, T, HD), BF16),
        V((H, 2, 2, NY, T, HD), BF16),
        V((H, 2, NY, T, HD), BF16),
        S((H, 2, NY - 1)), S((H, 2, NY - 1)), S((H, 2)),
        S((H, NY - 1)), S((H, NY - 1)), S((H,)),
        S((H, NY - 1)), S((H, NY - 1)), S((H,)),
        S((H, 2, NY)), S((H, 2, NY)), S((H, 2)), S((H, 2)),
        S((NY - 1,)), S((NY - 1,)), S((NZ - 1,)), S((NZ - 1,)),
        S((nb - 1,)), S((nb - 1,)), S((NY - 1,)), S((NY - 1,)),
        S((nb - 1,)), S((nb - 1,)), S((NY - 1,)), S((NY - 1,)),
        S((H, NY - 1)), S((H, NY - 1)), S((H,)),
        S((H, 2)), S((H, 2)), S((H, 2)), S((H, 2)),
        S((H, NY - 1)), S((H, NY - 1)), S((H,)),
        S((H, 2, NY - 1)), S((H, 2, NY - 1)), S((H, 2)),
    ]
    any_spec = pl.BlockSpec(memory_space=pl.ANY)
    smem = pl.BlockSpec(memory_space=pltpu.SMEM)
    loss, *grads = pl.pallas_call(
        functools.partial(kernel, nb, T),
        out_shape=(
            jax.ShapeDtypeStruct((1, 1), F32),
            jax.ShapeDtypeStruct((T, D), BF16),
            jax.ShapeDtypeStruct((T, D), BF16),
            jax.ShapeDtypeStruct(key_proj.shape, BF16),
            jax.ShapeDtypeStruct(key_proj.shape, BF16),
        ),
        in_specs=[smem, smem, any_spec, any_spec, any_spec, any_spec, pl.BlockSpec(memory_space=pltpu.VMEM)],
        out_specs=(smem, any_spec, any_spec, any_spec, any_spec),
        scratch_shapes=scratch,
        compiler_params=pltpu.CompilerParams(
            collective_id=0, has_side_effects=True, vmem_limit_bytes=56 * 1024 * 1024
        ),
        cost_estimate=pl.CostEstimate(flops=13 * 10**9, bytes_accessed=6 * 2**20, transcendentals=2**23),
        name="attention_backward",
    )(lengths, positives, residual, query_proj, key_proj, value_proj, norm_gain.reshape(NY, NG, HD))
    return loss.reshape(()), *own_buffers(grads)


def solution(mesh):
    rows = P(("batch", "seq"), None)
    return jax.shard_map(
        functools.partial(on_device, mesh.shape["batch"]),
        mesh=mesh,
        in_specs=(rows, rows, rows, rows, P(), P("batch"), P()),
        out_specs=(P(), rows, rows, rows, rows),
        check_vma=False,
    )
```

time: 156 us -> 213 us (1.37)
  the two profiles are of different devices: /device:TPU:26 before, /device:TPU:8 now
where the time goes in v2:
time: 213 us
  Pallas kernels  210 us (99%)
  between operations  2.98 us (1%)
    pallas_call x1, Pallas kernels, on_device(): pl.pallas_call(functools.partial(kernel, nb, T), out_shape=(jax.ShapeDtyp...  129 us
    pallas_call x1, Pallas kernels, own_buffers(): pl.pallas_call(functools.partial(copy_kernel, parts), out_shape=tuple((ja...  80.7 us

profile of v2, /device:TPU:8, one launch (start us, length us, event | category | flops | bytes accessed | tf_op | source)
XLA Modules:
  0.0 212.7 jit_solution(702726168950397154)
XLA Ops:
  1.3 129.1 %attention_backward.1 = (f32[1,1]{1,0:T(1,128)}, bf16[128,4096]{1,0:T(8,128)(2,1)}, bf16[128,4096]{1,0:T(8,128)(2,1)}, bf16[128,1024]{1,0:T(8,128)(2,1)}, bf16[128,1024]{1,0:T(8,128)(2,1)}) custom-call(s32[1]{0:T(128)S(6)} %copy.13.len_ref, s32[16]{0:T(128)} %pos_ref.1, bf16[128,4096]{1,0:T(8,128)(2,1)} %res_hbm.1, bf16[128,4096]{1,0:T(8,128)(2,1)} %q_hbm.1, ...), custom_call_target="tpu_custom_call" | custom-call | flops 12999999488 | bytes 6291456 | tf_op jit(solution)/shard_map/attention_backward/pallas_call | solution.py:595
  130.3 80.7 %copy_out.1 = (bf16[128,4096]{1,0:T(8,128)(2,1)}, bf16[128,4096]{1,0:T(8,128)(2,1)}, bf16[128,1024]{1,0:T(8,128)(2,1)}, bf16[128,1024]{1,0:T(8,128)(2,1)}) custom-call(bf16[128,4096]{1,0:T(8,128)(2,1)} %get-tuple-element.15.refs_0_, bf16[128,4096]{1,0:T(8,128)(2,1)} %get-tuple-element.16.refs_1_, bf16[128,1024]{1,0:T(8,128)(2,1)} %get-tuple-element.17.refs_2_, ...), custom_call_target="tpu_custom_call" | custom-call | bytes 5242880 | tf_op jit(solution)/shard_map/copy_out/pallas_call | solution.py:530

commit v3 on v2

--- a/solution.py
+++ b/solution.py
@@ -30,9 +30,9 @@
     nb, t_rows,
     len_ref, pos_ref, res_hbm, q_hbm, k_hbm, v_hbm, gain_ref,
     loss_ref, out_gr, out_gq, out_gk, out_gv,
-    kvb, kfx, kzt, vta, qin, qs, qt, est, mb, mrun, linv, acc, rin, smt,
+    k_buf, v_buf, q_buf, res_buf, kvb, kfx, kzt, vta, qin, qs, qt, est, mb, mrun, linv, acc, rin, smt,
     rsq, rsa, invr, pz, pza, emba, sga, lra, gbt, mrw, msa, mrc, dot_t, gro, dqa, gqo, dka, dva, dkvo, own, rs1, rs2, fin,
-    kvs, kvr, kvl, qss, qsr, qsl, rns, rnr, rnl, z1s, z1r, z2s, z2r,
+    lds, kvs, kvr, kvl, qss, qsr, qsl, rns, rnr, rnl, z1s, z1r, z2s, z2r,
     sqs, sqr, pzs, pzr, ems, emr, sis, sir, los, lor, mns, mnr,
     grs, grr, grl, r1s, r1r, r2s, r2r, gqs, gqr, gql, gks, gkr, gkl,
 ):
@@ -85,11 +85,12 @@
     length = len_ref[0]
     lenf = length.astype(F32)
 
-    for h in range(H):
-        for c, src in ((0, k_hbm), (1, v_hbm)):
-            lcopy(src.at[:, col(2 * y + h, HD)], kvb.at[h, 0, c, y], kvl.at[h, c]).start()
-        lcopy(q_hbm.at[:, col(2 * y + h, GW)], qin.at[h, y], qsl.at[h]).start()
-        lcopy(res_hbm.at[:, col(2 * y + h, GW)], rin.at[h, y], rnl.at[h]).start()
+    loads = [
+        lcopy(src, dst, lds.at[i])
+        for i, (src, dst) in enumerate(((k_hbm, k_buf), (v_hbm, v_buf), (q_hbm, q_buf), (res_hbm, res_buf)))
+    ]
+    for load in loads:
+        load.start()
 
     barrier = pltpu.get_barrier_semaphore()
     for k in range(1, NY):
@@ -100,23 +101,28 @@
         pl.semaphore_signal(barrier, inc=1, device_id=(bo(k), s), device_id_type=MESH)
     pl.semaphore_wait(barrier, NY - 1 + NZ - 1 + nb - 1)
 
+    for load in loads:
+        load.wait()
     for h in range(H):
+        for c, src in ((0, k_buf), (1, v_buf)):
+            lcopy(src.at[:, col(2 * y + h, HD)], kvb.at[h, 0, c, y], kvl.at[h, c]).start()
+            for k in (1, 3, 2):
+                yy = yo(k)
+                send(src.at[:, col(2 * yy + h, HD)], kvb.at[h, 0, c, y], kvs.at[h, c, k - 1], kvr.at[h, c, k - 1], ydev(yy))
+        lcopy(q_buf.at[:, col(2 * y + h, GW)], qin.at[h, y], qsl.at[h]).start()
         for k in (1, 3, 2):
             yy = yo(k)
-            for c, src in ((0, k_hbm), (1, v_hbm)):
-                send(src.at[:, col(2 * yy + h, HD)], kvb.at[h, 0, c, y], kvs.at[h, c, k - 1], kvr.at[h, c, k - 1], ydev(yy))
+            send(q_buf.at[:, col(2 * yy + h, GW)], qin.at[h, y], qss.at[h, k - 1], qsr.at[h, k - 1], ydev(yy))
+    for h in range(H):
+        lcopy(res_buf.at[:, col(2 * y + h, GW)], rin.at[h, y], rnl.at[h]).start()
         for k in (1, 3, 2):
             yy = yo(k)
-            send(q_hbm.at[:, col(2 * yy + h, GW)], qin.at[h, y], qss.at[h, k - 1], qsr.at[h, k - 1], ydev(yy))
-    for h in range(H):
-        for k in (1, 3, 2):
-            yy = yo(k)
-            send(res_hbm.at[:, col(2 * yy + h, GW)], rin.at[h, y], rns.at[h, k - 1], rnr.at[h, k - 1], ydev(yy))
+            send(res_buf.at[:, col(2 * yy + h, GW)], rin.at[h, y], rns.at[h, k - 1], rnr.at[h, k - 1], ydev(yy))
 
     for h in range(H):
         for k in (0, 1, 3, 2):
             p = yo(NY - k)
-            for c, src in ((0, k_hbm), (1, v_hbm)):
+            for c, src in ((0, k_buf), (1, v_buf)):
                 if k == 0:
                     lcopy(src.at[:, col(2 * y + h, HD)], kvb.at[h, 0, c, y], kvl.at[h, c]).wait()
                 else:
@@ -204,7 +210,7 @@
         def _():
             forward_hops(0)
 
-        await_columns(h, q_hbm, qin, qsl, qsr)
+        await_columns(h, q_buf, qin, qsl, qsr)
         prep_q(h)
         prep_kv(h, 0, zh)
         over_chunks(lambda yy: attend(h, 0, yy))
@@ -223,7 +229,7 @@
         return carry
 
     def far_step(h, carry):
-        await_columns(h, res_hbm, rin, rnl, rnr)
+        await_columns(h, res_buf, rin, rnl, rnr)
         prep_res(h)
         for way in range(2):
             await_ref(kvb.at[h, 3, :, pl.ds(2 * way, 2)], z2r.at[h, way])
@@ -508,31 +514,38 @@
             gq_send(h, k).wait_send()
 
 
-def copy_kernel(parts, *refs):
-    n = len(refs) // 2
-    sems = refs[-1]
-    copies = []
+def copy_kernel(parts, n, *refs):
+    srcs, dsts, bufs, sems = refs[:n], refs[n : 2 * n], refs[2 * n : 3 * n], refs[-1]
+    pairs = []
     for i in range(n):
-        src, dst = refs[i], refs[n + i]
-        rows = src.shape[0] // parts
+        rows = srcs[i].shape[0] // parts
         for p in range(parts):
             span = pl.ds(p * rows, rows)
-            copies.append(pltpu.make_async_copy(src.at[span], dst.at[span], sems.at[i, p]))
-    for copy in copies:
-        copy.start()
-    for copy in copies:
-        copy.wait()
+            pairs.append(
+                (
+                    pltpu.make_async_copy(srcs[i].at[span], bufs[i].at[span], sems.at[0, i, p]),
+                    pltpu.make_async_copy(bufs[i].at[span], dsts[i].at[span], sems.at[1, i, p]),
+                )
+            )
+    for load, _ in pairs:
+        load.start()
+    for load, give in pairs:
+        load.wait()
+        give.start()
+    for _, give in pairs:
+        give.wait()
 
 
 def own_buffers(arrays):
-    parts = 4
+    parts = 2
     any_spec = pl.BlockSpec(memory_space=pl.ANY)
     return pl.pallas_call(
-        functools.partial(copy_kernel, parts),
+        functools.partial(copy_kernel, parts, len(arrays)),
         out_shape=tuple(jax.ShapeDtypeStruct(x.shape, x.dtype) for x in arrays),
         in_specs=[any_spec] * len(arrays),
         out_specs=(any_spec,) * len(arrays),
-        scratch_shapes=[pltpu.SemaphoreType.DMA((len(arrays), parts))],
+        scratch_shapes=[pltpu.VMEM(x.shape, x.dtype) for x in arrays]
+        + [pltpu.SemaphoreType.DMA((2, len(arrays), parts))],
         compiler_params=pltpu.CompilerParams(vmem_limit_bytes=56 * 1024 * 1024),
         cost_estimate=pl.CostEstimate(flops=0, bytes_accessed=5 * 2**20, transcendentals=0),
         name="copy_out",
@@ -546,6 +559,7 @@
     S = pltpu.SemaphoreType.DMA
     columns = V((H, NY, T, GW), BF16)
     scratch = [
+        V(key_proj.shape, BF16), V(key_proj.shape, BF16), V((T, D), BF16), V((T, D), BF16),
         V((H, NZ, 2, NY, T, HD), BF16),
         V((H, NZ, BK, HD), BF16),
         V((H, NZ, HD, BK), BF16),
@@ -578,7 +592,7 @@
         V((H, 2, 2, 2, T, HD), BF16),
         V((H, 2, 2, NY, T, HD), BF16),
         V((H, 2, NY, T, HD), BF16),
-        S((H, 2, NY - 1)), S((H, 2, NY - 1)), S((H, 2)),
+        S((4,)), S((H, 2, NY - 1)), S((H, 2, NY - 1)), S((H, 2)),
         S((H, NY - 1)), S((H, NY - 1)), S((H,)),
         S((H, NY - 1)), S((H, NY - 1)), S((H,)),
         S((H, 2, NY)), S((H, 2, NY)), S((H, 2)), S((H, 2)),

time: 213 us -> 135 us (0.63)
  Pallas kernels: 210 us -> 132 us
    pallas_call x1, Pallas kernels: 80.7 us -> 2.66 us  [own_buffers(): pl.pallas_call(functools.partial(copy_kernel, parts, len(arrays)), out_sh...]
where the time goes in v3:
time: 135 us
  Pallas kernels  132 us (98%)
  between operations  2.98 us (2%)
    pallas_call x1, Pallas kernels, on_device(): pl.pallas_call(functools.partial(kernel, nb, T), out_shape=(jax.ShapeDtyp...  129 us

profile of v3, /device:TPU:8, one launch (start us, length us, event | category | flops | bytes accessed | tf_op | source)
XLA Modules:
  0.0 134.5 jit_solution(17347169972735150333)
XLA Ops:
  1.3 128.9 %attention_backward.1 = (f32[1,1]{1,0:T(1,128)}, bf16[128,4096]{1,0:T(8,128)(2,1)}, bf16[128,4096]{1,0:T(8,128)(2,1)}, bf16[128,1024]{1,0:T(8,128)(2,1)}, bf16[128,1024]{1,0:T(8,128)(2,1)}) custom-call(s32[1]{0:T(128)S(6)} %copy.13.len_ref, s32[16]{0:T(128)} %pos_ref.1, bf16[128,4096]{1,0:T(8,128)(2,1)} %res_hbm.1, bf16[128,4096]{1,0:T(8,128)(2,1)} %q_hbm.1, ...), custom_call_target="tpu_custom_call" | custom-call | flops 12999999488 | bytes 6291456 | tf_op jit(solution)/shard_map/attention_backward/pallas_call | solution.py:609
  130.2 2.7 %copy_out.1 = (bf16[128,4096]{1,0:T(8,128)(2,1)}, bf16[128,4096]{1,0:T(8,128)(2,1)}, bf16[128,1024]{1,0:T(8,128)(2,1)}, bf16[128,1024]{1,0:T(8,128)(2,1)}) custom-call(bf16[128,4096]{1,0:T(8,128)(2,1)} %get-tuple-element.15.refs_0_, bf16[128,4096]{1,0:T(8,128)(2,1)} %get-tuple-element.16.refs_1_, bf16[128,1024]{1,0:T(8,128)(2,1)} %get-tuple-element.17.refs_2_, ...), custom_call_target="tpu_custom_call" | custom-call | bytes 5242880 | tf_op jit(solution)/shard_map/copy_out/pallas_call | solution.py:542

commit v4 on v3

--- a/solution.py
+++ b/solution.py
@@ -152,7 +152,7 @@
             for j in range(G):
                 head = qin[h, yy, :, j * HD : (j + 1) * HD]
                 qs[h, yy, j * T : (j + 1) * T, :] = head
-                qt[h, yy, :, j * T : (j + 1) * T] = head.astype(F32).T.astype(BF16)
+                qt[h, yy, :, j * T : (j + 1) * T] = head.T
             mrun[h, yy] = jnp.full((1, G * T), -3e38, F32)
             acc[h, yy] = jnp.zeros((HD + 16, G * T), F32)
             return carry
@@ -162,7 +162,7 @@
     def prep_res(h):
         def body(yy, carry):
             for j in range(G):
-                smt[h, yy, :, j * T : (j + 1) * T] = rin[h, yy, :, j * HD : (j + 1) * HD].astype(F32).T
+                smt[h, yy, :, j * T : (j + 1) * T] = rin[h, yy, :, j * HD : (j + 1) * HD].T.astype(F32)
             return carry
 
         lax.fori_loop(0, NY, body, 0)
@@ -171,15 +171,15 @@
         first_key = kvb[h, rel, 0, 0, 0:1, :].astype(F32)
         for yy in range(NY):
             base = (yy * NZ + zb) * T
+            rows = slice(yy * T, (yy + 1) * T)
+            kp = kvb[h, rel, 0, yy]
             valid = lax.broadcasted_iota(jnp.int32, (T, HD), 0) + base < length
-            rows = slice(yy * T, (yy + 1) * T)
-            kp = kvb[h, rel, 0, yy].astype(F32)
-            vp = kvb[h, rel, 1, yy].astype(F32)
-            kfx[h, rel, rows, :] = jnp.where(valid, kp, first_key).astype(BF16)
-            kzt[h, rel, :, rows] = jnp.where(valid, kp, 0.0).T.astype(BF16)
-            vta[h, rel, 0:HD, rows] = jnp.where(valid, vp, 0.0).T.astype(BF16)
+            kfx[h, rel, rows, :] = jnp.where(valid, kp.astype(F32), first_key).astype(BF16)
             lanes = lax.broadcasted_iota(jnp.int32, (16, T), 1) + base < length
-            vta[h, rel, HD : HD + 16, rows] = jnp.where(lanes, 1.0, 0.0).astype(BF16)
+            ones = jnp.where(lanes, 1.0, 0.0).astype(BF16)
+            vta[h, rel, HD : HD + 16, rows] = ones
+            kzt[h, rel, :, rows] = kp.T * ones[0:1, :]
+            vta[h, rel, 0:HD, rows] = kvb[h, rel, 1, yy].T * ones[0:1, :]
 
     halves = [slice(part * (G * T // 2), (part + 1) * (G * T // 2)) for part in range(2)]
 
@@ -203,7 +203,7 @@
             body(yy)
             return carry
 
-        lax.fori_loop(0, NY, step, 0)
+        lax.fori_loop(0, NY, step, 0, unroll=2)
 
     def own_step(h, carry):
         @pl.when(h == 1)
@@ -359,16 +359,18 @@
 
     def pull_back(h, rel, yy):
         vals = kvb[h, rel, 1].reshape(BK, HD)
+        dos, scores = [], []
         for lanes in halves:
             r = jnp.exp2((mb[h, rel, yy, :, lanes] - mrun[h, yy, :, lanes]) * LOG2E_FACTOR) * linv[h, yy, :, lanes]
             do = (dot_t[h, yy, :, lanes].astype(F32) * r).astype(BF16)
             delta = jnp.sum(do.astype(F32) * acc[h, yy, 0:HD, lanes], axis=0, keepdims=True)
-            e = est[h, rel, yy, :, lanes]
             dp = dot(vals, do)
-            ds = (e.astype(F32) * (dp - delta)).astype(BF16)
-            dva[...] += dot(e, do, ((1,), (1,)))
-            dka[...] += dot(ds, qs[h, yy, lanes, :])
+            ds = est[h, rel, yy, :, lanes] * (dp - delta).astype(BF16)
             dqa[h, yy, :, lanes] += dot(kzt[h, rel], ds)
+            dos.append(do)
+            scores.append(ds)
+        dva[...] += dot(est[h, rel, yy], jnp.concatenate(dos, axis=1), ((1,), (1,)))
+        dka[...] += dot(jnp.concatenate(scores, axis=1), qs[h, yy])
 
     def clear():
         dka[...] = jnp.zeros((BK, HD), F32)
@@ -401,7 +403,7 @@
             kk = lax.rem(t + 1, NY)
             yy = yo(kk)
             for j in range(G):
-                gro[h, yy, :, j * HD : (j + 1) * HD] = dot_t[h, yy, :, j * T : (j + 1) * T].astype(F32).T.astype(BF16)
+                gro[h, yy, :, j * HD : (j + 1) * HD] = dot_t[h, yy, :, j * T : (j + 1) * T].T
 
             @pl.when(kk > 0)
             def _():
@@ -436,24 +438,26 @@
         clear()
 
         def chunk(t, carry):
-            kk = lax.rem(t + 1, NY)
-            yy = yo(kk)
-            pull_back(h, 0, yy)
-            for j in range(G):
-                part = dqa[h, yy, :, j * T : (j + 1) * T] * FACTOR
-                gqo[h, yy, :, j * HD : (j + 1) * HD] = part.T.astype(BF16)
-
-            @pl.when(kk > 0)
-            def _():
-                gq_send(h, kk).start()
-
-            @pl.when(kk == 0)
-            def _():
-                gq_local(h).start()
+            for u in range(2):
+                pull_back(h, 0, yo(lax.rem(2 * t + u + 1, NY)))
+            for u in range(2):
+                kk = lax.rem(2 * t + u + 1, NY)
+                yy = yo(kk)
+                for j in range(G):
+                    part = dqa[h, yy, :, j * T : (j + 1) * T] * FACTOR
+                    gqo[h, yy, :, j * HD : (j + 1) * HD] = part.astype(BF16).T
+
+                @pl.when(kk > 0)
+                def _(kk=kk):
+                    gq_send(h, kk).start()
+
+                @pl.when(kk == 0)
+                def _():
+                    gq_local(h).start()
 
             return carry
 
-        lax.fori_loop(0, NY, chunk, 0)
+        lax.fori_loop(0, NY // 2, chunk, 0)
         own[h, 0] = dka[...] * FACTOR
         own[h, 1] = dva[...]
         return carry

time: 135 us -> 133 us (0.985)
  Pallas kernels: 132 us -> 130 us
where the time goes in v4:
time: 133 us
  Pallas kernels  130 us (98%)
  between operations  2.98 us (2%)
    pallas_call x1, Pallas kernels, on_device(): pl.pallas_call(functools.partial(kernel, nb, T), out_shape=(jax.ShapeDtyp...  128 us

profile of v4, /device:TPU:8, one launch (start us, length us, event | category | flops | bytes accessed | tf_op | source)
XLA Modules:
  0.0 133.3 jit_solution(11506810629210613672)
XLA Ops:
  1.3 127.7 %attention_backward.1 = (f32[1,1]{1,0:T(1,128)}, bf16[128,4096]{1,0:T(8,128)(2,1)}, bf16[128,4096]{1,0:T(8,128)(2,1)}, bf16[128,1024]{1,0:T(8,128)(2,1)}, bf16[128,1024]{1,0:T(8,128)(2,1)}) custom-call(s32[1]{0:T(128)S(6)} %copy.13.len_ref, s32[16]{0:T(128)} %pos_ref.1, bf16[128,4096]{1,0:T(8,128)(2,1)} %res_hbm.1, bf16[128,4096]{1,0:T(8,128)(2,1)} %q_hbm.1, ...), custom_call_target="tpu_custom_call" | custom-call | flops 12999999488 | bytes 6291456 | tf_op jit(solution)/shard_map/attention_backward/pallas_call | solution.py:613
  128.9 2.7 %copy_out.1 = (bf16[128,4096]{1,0:T(8,128)(2,1)}, bf16[128,4096]{1,0:T(8,128)(2,1)}, bf16[128,1024]{1,0:T(8,128)(2,1)}, bf16[128,1024]{1,0:T(8,128)(2,1)}) custom-call(bf16[128,4096]{1,0:T(8,128)(2,1)} %get-tuple-element.15.refs_0_, bf16[128,4096]{1,0:T(8,128)(2,1)} %get-tuple-element.16.refs_1_, bf16[128,1024]{1,0:T(8,128)(2,1)} %get-tuple-element.17.refs_2_, ...), custom_call_target="tpu_custom_call" | custom-call | bytes 5242880 | tf_op jit(solution)/shard_map/copy_out/pallas_call | solution.py:546

commit v5 on v4

--- a/solution.py
+++ b/solution.py
@@ -103,32 +103,40 @@
 
     for load in loads:
         load.wait()
-    for h in range(H):
+    def kv_sends(h):
         for c, src in ((0, k_buf), (1, v_buf)):
             lcopy(src.at[:, col(2 * y + h, HD)], kvb.at[h, 0, c, y], kvl.at[h, c]).start()
             for k in (1, 3, 2):
                 yy = yo(k)
                 send(src.at[:, col(2 * yy + h, HD)], kvb.at[h, 0, c, y], kvs.at[h, c, k - 1], kvr.at[h, c, k - 1], ydev(yy))
+
+    def q_send(h, k):
+        yy = yo(k)
+        send(q_buf.at[:, col(2 * yy + h, GW)], qin.at[h, y], qss.at[h, k - 1], qsr.at[h, k - 1], ydev(yy))
+
+    def res_copy(h, k):
+        yy = yo(k)
+        return rcopy(res_buf.at[:, col(2 * yy + h, GW)], rin.at[h, y], rns.at[h, k - 1], rnr.at[h, k - 1], ydev(yy))
+
+    def hop1(h, k):
+        p = yo(NY - k)
+        for c, src in ((0, k_buf), (1, v_buf)):
+            if k == 0:
+                lcopy(src.at[:, col(2 * y + h, HD)], kvb.at[h, 0, c, y], kvl.at[h, c]).wait()
+            else:
+                await_ref(kvb.at[h, 0, c, p], kvr.at[h, c, k - 1])
+        send(kvb.at[h, 0, :, p], kvb.at[h, 1, :, p], z1s.at[h, 0, k], z1r.at[h, 0, k], right)
+        send(kvb.at[h, 0, :, p], kvb.at[h, 2, :, p], z1s.at[h, 1, k], z1r.at[h, 1, k], left)
+
+    kv_sends(0)
+    kv_sends(1)
+    for h in range(H):
         lcopy(q_buf.at[:, col(2 * y + h, GW)], qin.at[h, y], qsl.at[h]).start()
+        lcopy(res_buf.at[:, col(2 * y + h, GW)], rin.at[h, y], rnl.at[h]).start()
+        hop1(h, 0)
         for k in (1, 3, 2):
-            yy = yo(k)
-            send(q_buf.at[:, col(2 * yy + h, GW)], qin.at[h, y], qss.at[h, k - 1], qsr.at[h, k - 1], ydev(yy))
-    for h in range(H):
-        lcopy(res_buf.at[:, col(2 * y + h, GW)], rin.at[h, y], rnl.at[h]).start()
-        for k in (1, 3, 2):
-            yy = yo(k)
-            send(res_buf.at[:, col(2 * yy + h, GW)], rin.at[h, y], rns.at[h, k - 1], rnr.at[h, k - 1], ydev(yy))
-
-    for h in range(H):
-        for k in (0, 1, 3, 2):
-            p = yo(NY - k)
-            for c, src in ((0, k_buf), (1, v_buf)):
-                if k == 0:
-                    lcopy(src.at[:, col(2 * y + h, HD)], kvb.at[h, 0, c, y], kvl.at[h, c]).wait()
-                else:
-                    await_ref(kvb.at[h, 0, c, p], kvr.at[h, c, k - 1])
-            send(kvb.at[h, 0, :, p], kvb.at[h, 1, :, p], z1s.at[h, 0, k], z1r.at[h, 0, k], right)
-            send(kvb.at[h, 0, :, p], kvb.at[h, 2, :, p], z1s.at[h, 1, k], z1r.at[h, 1, k], left)
+            q_send(h, k)
+            hop1(h, k)
 
     def hop2(h, way):
         src, dev, piece = (1, right, 0) if way == 0 else (2, left, 2)
@@ -209,6 +217,8 @@
         @pl.when(h == 1)
         def _():
             forward_hops(0)
+            for k in (1, 3, 2):
+                res_copy(0, k).start()
 
         await_columns(h, q_buf, qin, qsl, qsr)
         prep_q(h)
@@ -223,6 +233,8 @@
         @pl.when(m == 2)
         def _():
             forward_hops(1)
+            for k in (1, 3, 2):
+                res_copy(1, k).start()
 
         prep_kv(h, rel, zo(5 - 2 * rel))
         over_chunks(lambda yy: attend(h, rel, yy))
@@ -514,6 +526,7 @@
             r1(h, way).wait_send()
             r2(h, way).wait_send()
         for k in range(1, NY):
+            res_copy(h, k).wait_send()
             gr_send(h, k).wait_send()
             gq_send(h, k).wait_send()
 

time: 133 us -> 132 us (level); the launches traced: 133 us -> 131 us
  Pallas kernels: 130 us -> 128 us
    pallas_call x1, Pallas kernels: 128 us -> 125 us  [on_device(): pl.pallas_call(functools.partial(kernel, nb, T), out_shape=(jax.ShapeDtyp...]
where the time goes in v5:
time: 132 us; the launch traced here: 131 us
  Pallas kernels  128 us (97%)
  between operations  2.98 us (2%)
    pallas_call x1, Pallas kernels, on_device(): pl.pallas_call(functools.partial(kernel, nb, T), out_shape=(jax.ShapeDtyp...  125 us
    pallas_call x1, Pallas kernels, own_buffers(): pl.pallas_call(functools.partial(copy_kernel, parts, len(arrays)), out_sh...  2.66 us

profile of v5, /device:TPU:8, one launch (start us, length us, event | category | flops | bytes accessed | tf_op | source)
XLA Modules:
  0.0 130.8 jit_solution(17038006234517557260)
XLA Ops:
  1.3 125.2 %attention_backward.1 = (f32[1,1]{1,0:T(1,128)}, bf16[128,4096]{1,0:T(8,128)(2,1)}, bf16[128,4096]{1,0:T(8,128)(2,1)}, bf16[128,1024]{1,0:T(8,128)(2,1)}, bf16[128,1024]{1,0:T(8,128)(2,1)}) custom-call(s32[1]{0:T(128)S(6)} %copy.13.len_ref, s32[16]{0:T(128)} %pos_ref.1, bf16[128,4096]{1,0:T(8,128)(2,1)} %res_hbm.1, bf16[128,4096]{1,0:T(8,128)(2,1)} %q_hbm.1, ...), custom_call_target="tpu_custom_call" | custom-call | flops 12999999488 | bytes 6291456 | tf_op jit(solution)/shard_map/attention_backward/pallas_call | solution.py:626
  126.5 2.7 %copy_out.1 = (bf16[128,4096]{1,0:T(8,128)(2,1)}, bf16[128,4096]{1,0:T(8,128)(2,1)}, bf16[128,1024]{1,0:T(8,128)(2,1)}, bf16[128,1024]{1,0:T(8,128)(2,1)}) custom-call(bf16[128,4096]{1,0:T(8,128)(2,1)} %get-tuple-element.15.refs_0_, bf16[128,4096]{1,0:T(8,128)(2,1)} %get-tuple-element.16.refs_1_, bf16[128,1024]{1,0:T(8,128)(2,1)} %get-tuple-element.17.refs_2_, ...), custom_call_target="tpu_custom_call" | custom-call | bytes 5242880 | tf_op jit(solution)/shard_map/copy_out/pallas_call | solution.py:559

commit v6 on v5

--- a/solution.py
+++ b/solution.py
@@ -347,13 +347,15 @@
     mean = sum_along_y(mrw, msa, mns, mnr) * invr[...] * (1.0 / (NY * NG * HD))
     mrw_scale = invr[...] * invr[...] * mean
 
-    def r1(h, way):
+    def r1(h, way, c):
         dev, piece = (right, 0) if way == 0 else (left, 2)
-        return rcopy(dkvo.at[h, 2, :, pl.ds(piece, 2)], rs1.at[h, way], r1s.at[h, way], r1r.at[h, way], dev)
-
-    def r2(h, way):
+        return rcopy(
+            dkvo.at[h, 2, c, pl.ds(piece, 2)], rs1.at[h, way, c], r1s.at[h, way, c], r1r.at[h, way, c], dev
+        )
+
+    def r2(h, way, c):
         dev = right if way == 0 else left
-        return rcopy(dkvo.at[h, 1 - way], rs2.at[h, way], r2s.at[h, way], r2r.at[h, way], dev)
+        return rcopy(dkvo.at[h, 1 - way, c], rs2.at[h, way, c], r2s.at[h, way, c], r2r.at[h, way, c], dev)
 
     def gq_send(h, kk):
         yy = yo(kk)
@@ -369,34 +371,42 @@
     def gr_local(h):
         return lcopy(gro.at[h, y], out_gr.at[:, col(2 * y + h, GW)], grl.at[h])
 
-    def pull_back(h, rel, yy):
+    def scaled_grads(h, rel, yy, lanes):
+        r = jnp.exp2((mb[h, rel, yy, :, lanes] - mrun[h, yy, :, lanes]) * LOG2E_FACTOR) * linv[h, yy, :, lanes]
+        return (dot_t[h, yy, :, lanes].astype(F32) * r).astype(BF16)
+
+    def values_back(h, rel, yy, dos=None):
+        if dos is None:
+            dos = [scaled_grads(h, rel, yy, lanes) for lanes in halves]
+        dva[...] += dot(est[h, rel, yy], jnp.concatenate(dos, axis=1), ((1,), (1,)))
+
+    def keys_back(h, rel, yy):
         vals = kvb[h, rel, 1].reshape(BK, HD)
         dos, scores = [], []
         for lanes in halves:
-            r = jnp.exp2((mb[h, rel, yy, :, lanes] - mrun[h, yy, :, lanes]) * LOG2E_FACTOR) * linv[h, yy, :, lanes]
-            do = (dot_t[h, yy, :, lanes].astype(F32) * r).astype(BF16)
+            do = scaled_grads(h, rel, yy, lanes)
             delta = jnp.sum(do.astype(F32) * acc[h, yy, 0:HD, lanes], axis=0, keepdims=True)
             dp = dot(vals, do)
             ds = est[h, rel, yy, :, lanes] * (dp - delta).astype(BF16)
             dqa[h, yy, :, lanes] += dot(kzt[h, rel], ds)
             dos.append(do)
             scores.append(ds)
-        dva[...] += dot(est[h, rel, yy], jnp.concatenate(dos, axis=1), ((1,), (1,)))
         dka[...] += dot(jnp.concatenate(scores, axis=1), qs[h, yy])
+        return dos
+
+    def pull_back(h, rel, yy):
+        values_back(h, rel, yy, keys_back(h, rel, yy))
 
     def clear():
         dka[...] = jnp.zeros((BK, HD), F32)
         dva[...] = jnp.zeros((BK, HD), F32)
 
-    def store(h, slot, added):
-        for c, ref in ((0, dka), (1, dva)):
-            for p in range(NY):
-                x = ref[p * T : (p + 1) * T, :]
-                if c == 0:
-                    x = x * FACTOR
-                if added is not None and p // 2 == added:
-                    x = x + rs1[h, added, c, p % 2].astype(F32)
-                dkvo[h, slot, c, p] = x.astype(BF16)
+    def store(h, slot, c, added):
+        for p in range(NY):
+            x = dva[p * T : (p + 1) * T, :] if c == 1 else dka[p * T : (p + 1) * T, :] * FACTOR
+            if added is not None and p // 2 == added:
+                x = x + rs1[h, added, c, p % 2].astype(F32)
+            dkvo[h, slot, c, p] = x.astype(BF16)
 
     def far_back(h, carry):
         for yy in range(NY):
@@ -406,10 +416,14 @@
             dot_t[h, yy] = (g * a - smt[h, yy] * c).astype(BF16)
             dqa[h, yy] = jnp.zeros((HD, G * T), F32)
         clear()
-        over_chunks(lambda yy: pull_back(h, 3, yy))
-        store(h, 2, None)
-        r1(h, 0).start()
-        r1(h, 1).start()
+        over_chunks(lambda yy: values_back(h, 3, yy))
+        store(h, 2, 1, None)
+        r1(h, 0, 1).start()
+        r1(h, 1, 1).start()
+        over_chunks(lambda yy: keys_back(h, 3, yy))
+        store(h, 2, 0, None)
+        r1(h, 0, 0).start()
+        r1(h, 1, 0).start()
 
         def give(t, carry):
             kk = lax.rem(t + 1, NY)
@@ -440,9 +454,10 @@
 
             @pl.when(way == w)
             def _(w=w):
-                await_ref(rs1.at[h, w], r1r.at[h, w])
-                store(h, 1 - w, w)
-                r2(h, w).start()
+                for c in (1, 0):
+                    await_ref(rs1.at[h, w, c], r1r.at[h, w, c])
+                    store(h, 1 - w, c, w)
+                    r2(h, w, c).start()
 
         return carry
 
@@ -484,8 +499,11 @@
     for k in range(1, nb):
         send(lra.at[b], lra.at[b], los.at[k - 1], lor.at[k - 1], (bo(k), s))
 
-    lax.fori_loop(0, 2 * H, near_back, 0)
-    lax.fori_loop(0, H, own_back, 0)
+    def finish_head(h, carry):
+        lax.fori_loop(2 * h, 2 * h + 2, near_back, 0)
+        return own_back(h, carry)
+
+    lax.fori_loop(0, H, finish_head, 0)
 
     for k in range(1, nb):
         await_ref(lra.at[bo(nb - k)], lor.at[k - 1])
@@ -495,14 +513,13 @@
     loss_ref[0, 0] = jnp.sum(loss) * (1.0 / (8 * HD * nb))
 
     for h in range(H):
-        await_ref(rs2.at[h, 0], r2r.at[h, 0])
-        await_ref(rs2.at[h, 1], r2r.at[h, 1])
-        for p in range(NY):
-            valid = lax.broadcasted_iota(jnp.int32, (T, HD), 0) + (p * NZ + zh) * T < length
-            for c in range(2):
+        for c, out in ((1, out_gv), (0, out_gk)):
+            await_ref(rs2.at[h, 0, c], r2r.at[h, 0, c])
+            await_ref(rs2.at[h, 1, c], r2r.at[h, 1, c])
+            for p in range(NY):
+                valid = lax.broadcasted_iota(jnp.int32, (T, HD), 0) + (p * NZ + zh) * T < length
                 x = own[h, c, p * T : (p + 1) * T, :] + rs2[h, 0, c, p].astype(F32) + rs2[h, 1, c, p].astype(F32)
                 fin[h, c, p] = jnp.where(valid, x, 0.0).astype(BF16)
-        for c, out in ((0, out_gk), (1, out_gv)):
             for k in (2, 1, 3):
                 yy = yo(k)
                 send(fin.at[h, c, yy], out.at[:, col(2 * y + h, HD)], gks.at[h, c, k - 1], gkr.at[h, c, k - 1], ydev(yy))
@@ -523,8 +540,9 @@
     for h in range(H):
         for way in range(2):
             hop2(h, way).wait_send()
-            r1(h, way).wait_send()
-            r2(h, way).wait_send()
+            for c in range(2):
+                r1(h, way, c).wait_send()
+                r2(h, way, c).wait_send()
         for k in range(1, NY):
             res_copy(h, k).wait_send()
             gr_send(h, k).wait_send()
@@ -617,7 +635,7 @@
         S((nb - 1,)), S((nb - 1,)), S((NY - 1,)), S((NY - 1,)),
         S((nb - 1,)), S((nb - 1,)), S((NY - 1,)), S((NY - 1,)),
         S((H, NY - 1)), S((H, NY - 1)), S((H,)),
-        S((H, 2)), S((H, 2)), S((H, 2)), S((H, 2)),
+        S((H, 2, 2)), S((H, 2, 2)), S((H, 2, 2)), S((H, 2, 2)),
         S((H, NY - 1)), S((H, NY - 1)), S((H,)),
         S((H, 2, NY - 1)), S((H, 2, NY - 1)), S((H, 2)),
     ]

time: 132 us -> 130 us (0.985)
  Pallas kernels: 128 us -> 125 us
    pallas_call x1, Pallas kernels: 125 us -> 123 us  [on_device(): pl.pallas_call(functools.partial(kernel, nb, T), out_shape=(jax.ShapeDtyp...]
where the time goes in v6:
time: 130 us; the launch traced here: 128 us
  Pallas kernels  125 us (96%)
  between operations  2.98 us (2%)
    pallas_call x1, Pallas kernels, on_device(): pl.pallas_call(functools.partial(kernel, nb, T), out_shape=(jax.ShapeDtyp...  123 us
    pallas_call x1, Pallas kernels, own_buffers(): pl.pallas_call(functools.partial(copy_kernel, parts, len(arrays)), out_sh...  2.66 us

profile of v6, /device:TPU:8, one launch (start us, length us, event | category | flops | bytes accessed | tf_op | source)
XLA Modules:
  0.0 128.2 jit_solution(2582676204847400496)
XLA Ops:
  1.3 122.6 %attention_backward.1 = (f32[1,1]{1,0:T(1,128)}, bf16[128,4096]{1,0:T(8,128)(2,1)}, bf16[128,4096]{1,0:T(8,128)(2,1)}, bf16[128,1024]{1,0:T(8,128)(2,1)}, bf16[128,1024]{1,0:T(8,128)(2,1)}) custom-call(s32[1]{0:T(128)S(6)} %copy.13.len_ref, s32[16]{0:T(128)} %pos_ref.1, bf16[128,4096]{1,0:T(8,128)(2,1)} %res_hbm.1, bf16[128,4096]{1,0:T(8,128)(2,1)} %q_hbm.1, ...), custom_call_target="tpu_custom_call" | custom-call | flops 12999999488 | bytes 6291456 | tf_op jit(solution)/shard_map/attention_backward/pallas_call | solution.py:644
  123.8 2.7 %copy_out.1 = (bf16[128,4096]{1,0:T(8,128)(2,1)}, bf16[128,4096]{1,0:T(8,128)(2,1)}, bf16[128,1024]{1,0:T(8,128)(2,1)}, bf16[128,1024]{1,0:T(8,128)(2,1)}) custom-call(bf16[128,4096]{1,0:T(8,128)(2,1)} %get-tuple-element.15.refs_0_, bf16[128,4096]{1,0:T(8,128)(2,1)} %get-tuple-element.16.refs_1_, bf16[128,1024]{1,0:T(8,128)(2,1)} %get-tuple-element.17.refs_2_, ...), custom_call_target="tpu_custom_call" | custom-call | bytes 5242880 | tf_op jit(solution)/shard_map/copy_out/pallas_call | solution.py:577

commit v7 on v6

--- a/solution.py
+++ b/solution.py
@@ -211,7 +211,7 @@
             body(yy)
             return carry
 
-        lax.fori_loop(0, NY, step, 0, unroll=2)
+        lax.fori_loop(0, NY, step, 0, unroll=NY)
 
     def own_step(h, carry):
         @pl.when(h == 1)
@@ -464,27 +464,19 @@
     def own_back(h, carry):
         clear()
 
-        def chunk(t, carry):
-            for u in range(2):
-                pull_back(h, 0, yo(lax.rem(2 * t + u + 1, NY)))
-            for u in range(2):
-                kk = lax.rem(2 * t + u + 1, NY)
-                yy = yo(kk)
-                for j in range(G):
-                    part = dqa[h, yy, :, j * T : (j + 1) * T] * FACTOR
-                    gqo[h, yy, :, j * HD : (j + 1) * HD] = part.astype(BF16).T
-
-                @pl.when(kk > 0)
-                def _(kk=kk):
-                    gq_send(h, kk).start()
-
-                @pl.when(kk == 0)
-                def _():
-                    gq_local(h).start()
-
-            return carry
-
-        lax.fori_loop(0, NY // 2, chunk, 0)
+        order = (2, 1, 3, 0)
+        for kk in order:
+            pull_back(h, 0, yo(kk))
+        for kk in order:
+            yy = yo(kk)
+            for j in range(G):
+                part = dqa[h, yy, :, j * T : (j + 1) * T] * FACTOR
+                gqo[h, yy, :, j * HD : (j + 1) * HD] = part.astype(BF16).T
+            if kk > 0:
+                gq_send(h, kk).start()
+            else:
+                gq_local(h).start()
+
         own[h, 0] = dka[...] * FACTOR
         own[h, 1] = dva[...]
         return carry

time: 130 us -> 128 us (0.985)
    pallas_call x1, Pallas kernels: 123 us -> 121 us  [on_device(): pl.pallas_call(functools.partial(kernel, nb, T), out_shape=(jax.ShapeDtyp...]
where the time goes in v7:
time: 128 us; the launch traced here: 127 us
  Pallas kernels  124 us (97%)
  between operations  2.98 us (2%)
    pallas_call x1, Pallas kernels, on_device(): pl.pallas_call(functools.partial(kernel, nb, T), out_shape=(jax.ShapeDtyp...  121 us
    pallas_call x1, Pallas kernels, own_buffers(): pl.pallas_call(functools.partial(copy_kernel, parts, len(arrays)), out_sh...  2.66 us

profile of v7, /device:TPU:8, one launch (start us, length us, event | category | flops | bytes accessed | tf_op | source)
XLA Modules:
  0.0 126.7 jit_solution(11590445874709792023)
XLA Ops:
  1.3 121.0 %attention_backward.1 = (f32[1,1]{1,0:T(1,128)}, bf16[128,4096]{1,0:T(8,128)(2,1)}, bf16[128,4096]{1,0:T(8,128)(2,1)}, bf16[128,1024]{1,0:T(8,128)(2,1)}, bf16[128,1024]{1,0:T(8,128)(2,1)}) custom-call(s32[1]{0:T(128)S(6)} %copy.13.len_ref, s32[16]{0:T(128)} %pos_ref.1, bf16[128,4096]{1,0:T(8,128)(2,1)} %res_hbm.1, bf16[128,4096]{1,0:T(8,128)(2,1)} %q_hbm.1, ...), custom_call_target="tpu_custom_call" | custom-call | flops 12999999488 | bytes 6291456 | tf_op jit(solution)/shard_map/attention_backward/pallas_call | solution.py:636
  122.3 2.7 %copy_out.1 = (bf16[128,4096]{1,0:T(8,128)(2,1)}, bf16[128,4096]{1,0:T(8,128)(2,1)}, bf16[128,1024]{1,0:T(8,128)(2,1)}, bf16[128,1024]{1,0:T(8,128)(2,1)}) custom-call(bf16[128,4096]{1,0:T(8,128)(2,1)} %get-tuple-element.15.refs_0_, bf16[128,4096]{1,0:T(8,128)(2,1)} %get-tuple-element.16.refs_1_, bf16[128,1024]{1,0:T(8,128)(2,1)} %get-tuple-element.17.refs_2_, ...), custom_call_target="tpu_custom_call" | custom-call | bytes 5242880 | tf_op jit(solution)/shard_map/copy_out/pallas_call | solution.py:569

commit v8 on v7

--- a/solution.py
+++ b/solution.py
@@ -34,7 +34,7 @@
     rsq, rsa, invr, pz, pza, emba, sga, lra, gbt, mrw, msa, mrc, dot_t, gro, dqa, gqo, dka, dva, dkvo, own, rs1, rs2, fin,
     lds, kvs, kvr, kvl, qss, qsr, qsl, rns, rnr, rnl, z1s, z1r, z2s, z2r,
     sqs, sqr, pzs, pzr, ems, emr, sis, sir, los, lor, mns, mnr,
-    grs, grr, grl, r1s, r1r, r2s, r2r, gqs, gqr, gql, gks, gkr, gkl,
+    grs, grr, grl, r1s, r1r, r2s, r2r, gqs, gqr, gql, gks, gkr, gkl, rly, rys, ryr, rfs, rfr,
 ):
     T = t_rows
     BK = NY * T
@@ -75,6 +75,38 @@
     def await_ref(ref, sem):
         pltpu.make_async_copy(ref, ref, sem).wait()
 
+    def half_rows(way):
+        return pl.ds(way * (T // 2), T // 2)
+
+    def relay_out(t, h, way, src):
+        dev = ydev(yo(1 if way == 0 else NY - 1))
+        return rcopy(src, rly.at[t, h, way], rys.at[t, h, way], ryr.at[t, h, way], dev)
+
+    def relay_on(t, h, way, dst):
+        dev = ydev(yo(1 if way == 0 else NY - 1))
+        return rcopy(rly.at[t, h, way], dst, rfs.at[t, h, way], rfr.at[t, h, way], dev)
+
+    def relay(t, h, place):
+        for way in range(2):
+            await_ref(rly.at[t, h, way], ryr.at[t, h, way])
+            relay_on(t, h, way, place(h, yo(NY - 1 if way == 0 else 1), half_rows(way))).start()
+
+    def await_relayed(t, h, place):
+        for way in range(2):
+            await_ref(place(h, yo(2), half_rows(way)), rfr.at[t, h, way])
+
+    def q_place(h, yy, rows):
+        return qin.at[h, yy, rows]
+
+    def res_place(h, yy, rows):
+        return rin.at[h, yy, rows]
+
+    def gr_place(h, yy, rows):
+        return out_gr.at[rows, col(2 * yy + h, GW)]
+
+    def gq_place(h, yy, rows):
+        return out_gq.at[rows, col(2 * yy + h, GW)]
+
     sends = []
 
     def send(src, dst, ssem, rsem, dev):
@@ -112,11 +144,21 @@
 
     def q_send(h, k):
         yy = yo(k)
+        if k == 2:
+            for way in range(2):
+                relay_out(0, h, way, q_buf.at[half_rows(way), col(2 * yy + h, GW)]).start()
+            return
         send(q_buf.at[:, col(2 * yy + h, GW)], qin.at[h, y], qss.at[h, k - 1], qsr.at[h, k - 1], ydev(yy))
 
     def res_copy(h, k):
         yy = yo(k)
         return rcopy(res_buf.at[:, col(2 * yy + h, GW)], rin.at[h, y], rns.at[h, k - 1], rnr.at[h, k - 1], ydev(yy))
+
+    def res_sends(h):
+        for k in (1, 3):
+            res_copy(h, k).start()
+        for way in range(2):
+            relay_out(1, h, way, res_buf.at[half_rows(way), col(2 * yo(2) + h, GW)]).start()
 
     def hop1(h, k):
         p = yo(NY - k)
@@ -138,6 +180,8 @@
             q_send(h, k)
             hop1(h, k)
 
+    relay(0, 0, q_place)
+
     def hop2(h, way):
         src, dev, piece = (1, right, 0) if way == 0 else (2, left, 2)
         return rcopy(
@@ -150,10 +194,11 @@
                 await_ref(kvb.at[h, 1 + way, :, yo(NY - k)], z1r.at[h, way, k])
             hop2(h, way).start()
 
-    def await_columns(h, src, dst, lsem, rsem):
+    def await_columns(t, h, src, dst, lsem, rsem, place):
         lcopy(src.at[:, col(2 * y + h, GW)], dst.at[h, y], lsem.at[h]).wait()
-        for k in range(1, NY):
+        for k in (1, 3):
             await_ref(dst.at[h, yo(NY - k)], rsem.at[h, k - 1])
+        await_relayed(t, h, place)
 
     def prep_q(h):
         def body(yy, carry):
@@ -217,12 +262,16 @@
         @pl.when(h == 1)
         def _():
             forward_hops(0)
-            for k in (1, 3, 2):
-                res_copy(0, k).start()
-
-        await_columns(h, q_buf, qin, qsl, qsr)
+            res_sends(0)
+
+        await_columns(0, h, q_buf, qin, qsl, qsr, q_place)
         prep_q(h)
         prep_kv(h, 0, zh)
+
+        @pl.when(h == 0)
+        def _():
+            relay(0, 1, q_place)
+
         over_chunks(lambda yy: attend(h, 0, yy))
         return carry
 
@@ -233,15 +282,19 @@
         @pl.when(m == 2)
         def _():
             forward_hops(1)
-            for k in (1, 3, 2):
-                res_copy(1, k).start()
+            res_sends(1)
+            relay(1, 0, res_place)
 
         prep_kv(h, rel, zo(5 - 2 * rel))
         over_chunks(lambda yy: attend(h, rel, yy))
         return carry
 
     def far_step(h, carry):
-        await_columns(h, res_buf, rin, rnl, rnr)
+        @pl.when(h == 0)
+        def _():
+            relay(1, 1, res_place)
+
+        await_columns(1, h, res_buf, rin, rnl, rnr, res_place)
         prep_res(h)
         for way in range(2):
             await_ref(kvb.at[h, 3, :, pl.ds(2 * way, 2)], z2r.at[h, way])
@@ -425,29 +478,33 @@
         r1(h, 0, 0).start()
         r1(h, 1, 0).start()
 
-        def give(t, carry):
-            kk = lax.rem(t + 1, NY)
+        for kk in (2, 1, 3, 0):
             yy = yo(kk)
             for j in range(G):
                 gro[h, yy, :, j * HD : (j + 1) * HD] = dot_t[h, yy, :, j * T : (j + 1) * T].T
-
-            @pl.when(kk > 0)
-            def _():
+            if kk == 2:
+                for way in range(2):
+                    relay_out(2, h, way, gro.at[h, yy, half_rows(way)]).start()
+            elif kk > 0:
                 gr_send(h, kk).start()
-
-            @pl.when(kk == 0)
-            def _():
+            else:
                 gr_local(h).start()
-
-            return carry
-
-        lax.fori_loop(0, NY, give, 0)
         return carry
 
     def near_back(m, carry):
         h = lax.div(m, 2)
         way = lax.rem(m, 2)
         rel = 2 - way
+
+        @pl.when(m == 2)
+        def _():
+            relay(2, 0, gr_place)
+
+        @pl.when(m == 3)
+        def _():
+            relay(2, 1, gr_place)
+            relay(3, 0, gq_place)
+
         clear()
         over_chunks(lambda yy: pull_back(h, rel, yy))
         for w in range(2):
@@ -472,7 +529,10 @@
             for j in range(G):
                 part = dqa[h, yy, :, j * T : (j + 1) * T] * FACTOR
                 gqo[h, yy, :, j * HD : (j + 1) * HD] = part.astype(BF16).T
-            if kk > 0:
+            if kk == 2:
+                for way in range(2):
+                    relay_out(3, h, way, gqo.at[h, yy, half_rows(way)]).start()
+            elif kk > 0:
                 gq_send(h, kk).start()
             else:
                 gq_local(h).start()
@@ -505,6 +565,8 @@
     loss_ref[0, 0] = jnp.sum(loss) * (1.0 / (8 * HD * nb))
 
     for h in range(H):
+        if h == H - 1:
+            relay(3, h, gq_place)
         for c, out in ((1, out_gv), (0, out_gk)):
             await_ref(rs2.at[h, 0, c], r2r.at[h, 0, c])
             await_ref(rs2.at[h, 1, c], r2r.at[h, 1, c])
@@ -520,9 +582,11 @@
     for h in range(H):
         gq_local(h).wait()
         gr_local(h).wait()
-        for k in range(1, NY):
+        for k in (1, 3):
             await_ref(out_gr.at[:, col(2 * yo(NY - k) + h, GW)], grr.at[h, k - 1])
             await_ref(out_gq.at[:, col(2 * yo(NY - k) + h, GW)], gqr.at[h, k - 1])
+        await_relayed(2, h, gr_place)
+        await_relayed(3, h, gq_place)
         for c, out in ((0, out_gk), (1, out_gv)):
             lcopy(fin.at[h, c, y], out.at[:, col(2 * y + h, HD)], gkl.at[h, c]).wait()
             for k in range(1, NY):
@@ -535,7 +599,10 @@
             for c in range(2):
                 r1(h, way, c).wait_send()
                 r2(h, way, c).wait_send()
-        for k in range(1, NY):
+            for t in range(4):
+                relay_out(t, h, way, rly.at[t, h, way]).wait_send()
+                relay_on(t, h, way, rly.at[t, h, way]).wait_send()
+        for k in (1, 3):
             res_copy(h, k).wait_send()
             gr_send(h, k).wait_send()
             gq_send(h, k).wait_send()
@@ -630,6 +697,8 @@
         S((H, 2, 2)), S((H, 2, 2)), S((H, 2, 2)), S((H, 2, 2)),
         S((H, NY - 1)), S((H, NY - 1)), S((H,)),
         S((H, 2, NY - 1)), S((H, 2, NY - 1)), S((H, 2)),
+        V((4, H, 2, T // 2, GW), BF16),
+        S((4, H, 2)), S((4, H, 2)), S((4, H, 2)), S((4, H, 2)),
     ]
     any_spec = pl.BlockSpec(memory_space=pl.ANY)
     smem = pl.BlockSpec(memory_space=pltpu.SMEM)

time: 128 us -> 130 us (1.016)
  no operation moved by 1% of the time
where the time goes in v8:
time: 130 us; the launch traced here: 128 us
  Pallas kernels  125 us (96%)
  between operations  2.98 us (2%)
    pallas_call x1, Pallas kernels, on_device(): pl.pallas_call(functools.partial(kernel, nb, T), out_shape=(jax.ShapeDtyp...  122 us
    pallas_call x1, Pallas kernels, own_buffers(): pl.pallas_call(functools.partial(copy_kernel, parts, len(arrays)), out_sh...  2.66 us

profile of v8, /device:TPU:8, one launch (start us, length us, event | category | flops | bytes accessed | tf_op | source)
XLA Modules:
  0.0 127.8 jit_solution(2089298066195532911)
XLA Ops:
  1.3 122.2 %attention_backward.1 = (f32[1,1]{1,0:T(1,128)}, bf16[128,4096]{1,0:T(8,128)(2,1)}, bf16[128,4096]{1,0:T(8,128)(2,1)}, bf16[128,1024]{1,0:T(8,128)(2,1)}, bf16[128,1024]{1,0:T(8,128)(2,1)}) custom-call(s32[1]{0:T(128)S(6)} %copy.13.len_ref, s32[16]{0:T(128)} %pos_ref.1, bf16[128,4096]{1,0:T(8,128)(2,1)} %res_hbm.1, bf16[128,4096]{1,0:T(8,128)(2,1)} %q_hbm.1, ...), custom_call_target="tpu_custom_call" | custom-call | flops 12999999488 | bytes 6291456 | tf_op jit(solution)/shard_map/attention_backward/pallas_call | solution.py:705
  123.4 2.7 %copy_out.1 = (bf16[128,4096]{1,0:T(8,128)(2,1)}, bf16[128,4096]{1,0:T(8,128)(2,1)}, bf16[128,1024]{1,0:T(8,128)(2,1)}, bf16[128,1024]{1,0:T(8,128)(2,1)}) custom-call(bf16[128,4096]{1,0:T(8,128)(2,1)} %get-tuple-element.15.refs_0_, bf16[128,4096]{1,0:T(8,128)(2,1)} %get-tuple-element.16.refs_1_, bf16[128,1024]{1,0:T(8,128)(2,1)} %get-tuple-element.17.refs_2_, ...), custom_call_target="tpu_custom_call" | custom-call | bytes 5242880 | tf_op jit(solution)/shard_map/copy_out/pallas_call | solution.py:636

commit v9 on v7

--- a/solution.py
+++ b/solution.py
@@ -464,11 +464,9 @@
     def own_back(h, carry):
         clear()
 
-        order = (2, 1, 3, 0)
-        for kk in order:
-            pull_back(h, 0, yo(kk))
-        for kk in order:
+        for kk in (2, 1, 3, 0):
             yy = yo(kk)
+            pull_back(h, 0, yy)
             for j in range(G):
                 part = dqa[h, yy, :, j * T : (j + 1) * T] * FACTOR
                 gqo[h, yy, :, j * HD : (j + 1) * HD] = part.astype(BF16).T

time: 128 us -> 128 us (level)
  the two profiles are of different devices: /device:TPU:8 before, /device:TPU:36 now
where the time goes in v9:
time: 128 us
  Pallas kernels  125 us (98%)
  between operations  2.98 us (2%)
    pallas_call x1, Pallas kernels, on_device(): pl.pallas_call(functools.partial(kernel, nb, T), out_shape=(jax.ShapeDtyp...  122 us
    pallas_call x1, Pallas kernels, own_buffers(): pl.pallas_call(functools.partial(copy_kernel, parts, len(arrays)), out_sh...  2.66 us

profile of v9, /device:TPU:36, one launch (start us, length us, event | category | flops | bytes accessed | tf_op | source)
XLA Modules:
  0.0 128.0 jit_solution(18180767567192826551)
XLA Ops:
  1.3 122.4 %attention_backward.1 = (f32[1,1]{1,0:T(1,128)}, bf16[128,4096]{1,0:T(8,128)(2,1)}, bf16[128,4096]{1,0:T(8,128)(2,1)}, bf16[128,1024]{1,0:T(8,128)(2,1)}, bf16[128,1024]{1,0:T(8,128)(2,1)}) custom-call(s32[1]{0:T(128)S(6)} %copy.13.len_ref, s32[16]{0:T(128)} %pos_ref.1, bf16[128,4096]{1,0:T(8,128)(2,1)} %res_hbm.1, bf16[128,4096]{1,0:T(8,128)(2,1)} %q_hbm.1, ...), custom_call_target="tpu_custom_call" | custom-call | flops 12999999488 | bytes 6291456 | tf_op jit(solution)/shard_map/attention_backward/pallas_call | solution.py:634
  123.7 2.7 %copy_out.1 = (bf16[128,4096]{1,0:T(8,128)(2,1)}, bf16[128,4096]{1,0:T(8,128)(2,1)}, bf16[128,1024]{1,0:T(8,128)(2,1)}, bf16[128,1024]{1,0:T(8,128)(2,1)}) custom-call(bf16[128,4096]{1,0:T(8,128)(2,1)} %get-tuple-element.15.refs_0_, bf16[128,4096]{1,0:T(8,128)(2,1)} %get-tuple-element.16.refs_1_, bf16[128,1024]{1,0:T(8,128)(2,1)} %get-tuple-element.17.refs_2_, ...), custom_call_target="tpu_custom_call" | custom-call | bytes 5242880 | tf_op jit(solution)/shard_map/copy_out/pallas_call | solution.py:567
